TPU v7x, 128 devices: a whole 4x4x4 slice. The times are simulated.
128 devices in a mesh: shard: 2 (over x_hi), blk: 4 (over x_lo, core), aa: 16 (over z, y).
Axes of the slice: x: 4 (x_hi: 2, x_lo: 2; x = x_hi * 2 + x_lo), y: 4, z: 4, core: 2. Of those that a mesh axis runs over, the one named last changes fastest.
Arguments:
- tokens: bfloat16 [2, 8192, 1024], P('shard', ('blk', 'aa')), may hold values from -16 to 16
- segments: int32 [2, 8192], P('shard'), may hold values from 0 to 34, as said below
- valid: int32 [2, 8192], P('shard'), may hold values from 0 to 1, as said below
- w_query: bfloat16 [1024, 1024], P('shard'), may hold values from -0.1875 to 0.1875
- w_key: bfloat16 [1024, 1024], P('shard'), may hold values from -0.1875 to 0.1875
- w_value: bfloat16 [1024, 1024], P('shard'), may hold values from -0.1875 to 0.1875
- w_out: bfloat16 [1024, 1024], P('shard'), may hold values from -6 to 6
- norm1_gain: bfloat16 [1024], P('shard'), may hold values from 0.5 to 1.5
- norm1_bias: bfloat16 [1024], P('shard'), may hold values from -3 to 3
- w_in: bfloat16 [1024, 4096], P('shard'), may hold values from -0.1875 to 0.1875
- w_down: bfloat16 [4096, 1024], P('shard'), may hold values from -0.09375 to 0.09375
- norm2_gain: bfloat16 [1024], P('shard'), may hold values from 0.5 to 1.5
- norm2_bias: bfloat16 [1024], P('shard'), may hold values from -3 to 3
- cotangent: bfloat16 [2, 8192, 1024], P('shard', ('blk', 'aa')), may hold values from -6 to 6
Outputs:
- output: bfloat16 [2, 8192, 1024], P('shard', ('blk', 'aa'))
- grad_tokens: bfloat16 [2, 8192, 1024], P('shard', ('blk', 'aa'))
- grad_w_query: float32 [1024, 1024], P('shard')
- grad_w_key: float32 [1024, 1024], P('shard')
- grad_w_value: float32 [1024, 1024], P('shard')
- grad_w_out: float32 [1024, 1024], P('shard')
- grad_norm1_gain: float32 [1024], P('shard')
- grad_norm1_bias: float32 [1024], P('shard')
- grad_w_in: float32 [1024, 4096], P('shard')
- grad_w_down: float32 [4096, 1024], P('shard')
- grad_norm2_gain: float32 [1024], P('shard')
- grad_norm2_bias: float32 [1024], P('shard')
Inputs may be any that keep to these rules, and one draw needn't show every extreme that they name: `segments`: segment numbers never fall along a sequence and start at 0. In each sequence one document begins in the first quarter and ends in the last quarter of the sequence; every other document holds at most 2048 tokens. Padding positions all carry the number 34. `valid`: each sequence is 1 on a prefix and 0 on a tail of at least 256 tokens and fewer than 1024.
All inputs are finite; a program needn't handle non-finite values.
Results may differ from a plain program's by a relative error of at most 0.035.
Values may be sent and summed in bfloat16 or wider, within the bound.
A program may use at most 256 MiB of HBM per device.

v0:
```python
import math

import jax
import jax.numpy as jnp
from jax import lax
from jax.sharding import PartitionSpec as P

HEADS = 16
HEAD = 64
QBLK = 512


MASKED_SCORE = -1e30
NORM_EPSILON = 1e-05


def from_behind(value, axis, by):
    devices = lax.axis_size(axis)
    return lax.ppermute(value, axis, [(i, (i + by) % devices) for i in range(devices)])


def sent_together(arrays, axis, dim, along):
    widths = [math.prod(a.shape[along:]) for a in arrays]
    both = jnp.concatenate(
        [a.reshape(*a.shape[:along], w) for a, w in zip(arrays, widths)], axis=along
    )
    filled = lax.all_gather(both, axis, axis=dim, tiled=True)
    pieces = jnp.split(filled, [sum(widths[:k]) for k in range(1, len(widths))], axis=along)
    return tuple(
        (b.reshape(*filled.shape[:along], *a.shape[along:]) for a, b in zip(arrays, pieces))
    )


def side_by_side(arrays, axis, dim, along):
    columns = [a.reshape(*a.shape[:along], -1) for a in arrays]
    both = jnp.concatenate(columns, axis=along)
    filled, at, gathered = (lax.psum_scatter(both, axis, scatter_dimension=dim, tiled=True), 0, [])
    for a, column in zip(arrays, columns):
        piece = filled[..., at : at + column.shape[along]]
        gathered.append(piece.reshape(*piece.shape[:along], *a.shape[along:]))
        at += column.shape[along]
    return tuple(gathered)


def split_up(value, dim, devices):
    before, after = (value.shape[:dim], value.shape[dim + 1 :])
    return jnp.moveaxis(value.reshape(*before, devices, -1, *after), dim, 0)


def one_scatter(arrays, axis, dims):
    devices = lax.axis_size(axis)
    pieces = [split_up(a, dim, devices) for a, dim in zip(arrays, dims)]
    lines = jnp.concatenate([b.reshape(devices, -1) for b in pieces], axis=1)
    span = max(16, -(-lines.shape[1] // 1024) * 8)
    lines = jnp.pad(lines, ((0, 0), (0, span * 128 - lines.shape[1]))).reshape(-1, 128)
    flat, at, gathered = (lax.psum_scatter(lines, axis, tiled=True).reshape(-1), 0, [])
    for b in pieces:
        part = b[0]
        gathered.append(flat[at : at + part.size].reshape(part.shape))
        at += part.size
    return tuple(gathered)


def normalize(summed_in, norm_gain, norm_bias):
    row_mean = jnp.mean(summed_in, axis=-1, keepdims=True)
    centred = summed_in - row_mean
    inv_std = lax.rsqrt(jnp.mean(centred * centred, axis=-1, keepdims=True) + NORM_EPSILON)
    scaled = centred * inv_std
    return (scaled * norm_gain + norm_bias, scaled, inv_std)


def normalize_back(upstream, scaled, inv_std, norm_gain):
    weighted = upstream * norm_gain
    centred = weighted - jnp.mean(weighted, axis=-1, keepdims=True)
    result = inv_std * (centred - scaled * jnp.mean(weighted * scaled, axis=-1, keepdims=True))
    return (result, jnp.sum(upstream * scaled, axis=0), jnp.sum(upstream, axis=0))


def exact_gelu(values):
    return jax.nn.gelu(values, approximate=False)


def allowed_mask(segments, valid, query_start, key_start, query_count, key_count):
    seg_query = lax.dynamic_slice_in_dim(segments, query_start, query_count)
    seg_key = lax.dynamic_slice_in_dim(segments, key_start, key_count)
    live_key = lax.dynamic_slice_in_dim(valid, key_start, key_count)
    place_query = query_start + jnp.arange(query_count, dtype=jnp.int32)
    place_key = key_start + jnp.arange(key_count, dtype=jnp.int32)
    same_doc = (seg_query[:, None] == seg_key[None, :]) & (live_key[None, :] == 1)
    return same_doc | (place_query[:, None] == place_key[None, :])


def pass_keys(kv_pair):
    return from_behind(kv_pair, "blk", 1)


def pass_grads(grad_pair):
    return from_behind(grad_pair.astype(jnp.bfloat16), "blk", 1).astype(grad_pair.dtype)


def shards(
    tokens,
    segments,
    valid,
    w_query,
    w_key,
    w_value,
    w_out,
    norm1_gain,
    norm1_bias,
    w_in,
    w_down,
    norm2_gain,
    norm2_bias,
    cotangent,
):
    gathered = (
        *sent_together(
            (w_query, w_key, w_value, w_out, norm1_gain, norm1_bias, w_in), "shard", 0, 1
        ),
        lax.all_gather(w_down, "shard", axis=0, tiled=True),
        lax.all_gather(norm2_gain, "shard", axis=0, tiled=True),
        lax.all_gather(norm2_bias, "shard", axis=0, tiled=True),
    )
    (
        full_query,
        full_key,
        full_value,
        full_out,
        gain_one,
        bias_one,
        full_in,
        full_down,
        gain_two,
        bias_two,
    ) = gathered
    gain_one = gain_one.astype(jnp.float32)
    bias_one = bias_one.astype(jnp.float32)
    gain_two = gain_two.astype(jnp.float32)
    bias_two = bias_two.astype(jnp.float32)
    token_rows = tokens[0]
    seq_segments = segments[0]
    seq_valid = valid[0]
    tok_rows, width = token_rows.shape
    groups = lax.axis_size("aa")
    head_local = HEADS // groups
    group_width = head_local * HEAD
    block_len = groups * tok_rows
    block_count = block_len // QBLK
    score_scale = HEAD ** (-0.5)
    cycle_size = lax.axis_size("blk")
    cycle_index = lax.axis_index("blk")
    query_base = cycle_index * block_len
    block_ids = jnp.arange(block_count, dtype=jnp.int32)
    projected = [
        jnp.dot(token_rows, matrix, preferred_element_type=jnp.float32)
        .astype(jnp.bfloat16)
        .reshape(tok_rows, groups, group_width)
        for matrix in (full_query, full_key, full_value)
    ]
    heads_all = lax.all_to_all(
        jnp.concatenate(projected, axis=2), "aa", split_axis=1, concat_axis=0, tiled=True
    )
    heads_all = heads_all.reshape(block_len, 3, head_local, HEAD)
    q_blocks = heads_all[:, 0].reshape(block_count, QBLK, head_local, HEAD)
    kv_pair = heads_all[:, 1:]
    state = (
        jnp.full((block_count, head_local, QBLK), MASKED_SCORE, jnp.float32),
        jnp.zeros((block_count, head_local, QBLK), jnp.float32),
        jnp.zeros((block_count, QBLK, head_local, HEAD), jnp.float32),
    )
    kept_pairs = []
    for cycle_step in range(cycle_size):
        if cycle_step > 0:
            kv_pair = pass_keys(kv_pair)
        kept_pairs.append(kv_pair)
        key_start = (cycle_index - cycle_step) % cycle_size * block_len
        attend_key_heads = kv_pair[:, 0]
        attend_value_heads = kv_pair[:, 1]

        def attend_visit(inputs):
            block_index, query_block, running_max, running_sum, summed = inputs
            allowed = allowed_mask(
                seq_segments, seq_valid, query_base + block_index * QBLK, key_start, QBLK, block_len
            )
            scores = (
                jnp.einsum(
                    "qhd,khd->hqk",
                    query_block,
                    attend_key_heads,
                    preferred_element_type=jnp.float32,
                )
                * score_scale
            )
            scores = jnp.where(allowed[None], scores, MASKED_SCORE)
            new_max = jnp.maximum(running_max, jnp.max(scores, axis=-1))
            factor = jnp.exp(running_max - new_max)
            weights_new = jnp.exp(scores - new_max[..., None])
            new_sum = running_sum * factor + jnp.sum(weights_new, axis=-1)
            new_summed = summed * jnp.transpose(factor)[..., None] + jnp.einsum(
                "hqk,khd->qhd",
                weights_new.astype(jnp.bfloat16),
                attend_value_heads,
                preferred_element_type=jnp.float32,
            )
            return (new_max, new_sum, new_summed)

        state = lax.map(attend_visit, (block_ids, q_blocks) + state)
    running_max, running_sum, summed = state
    attn_heads = summed / jnp.transpose(running_sum, (0, 2, 1))[..., None]
    log_total = running_max + jnp.log(running_sum)
    mixed = lax.all_to_all(
        attn_heads.astype(jnp.bfloat16).reshape(block_len, 1, group_width),
        "aa",
        split_axis=0,
        concat_axis=1,
        tiled=True,
    ).reshape(tok_rows, width)
    attn = jnp.dot(mixed, full_out, preferred_element_type=jnp.float32)
    first, scaled_one, inv_one = normalize(
        token_rows.astype(jnp.float32) + attn, gain_one, bias_one
    )
    first_low = first.astype(jnp.bfloat16)
    pre = jnp.dot(first_low, full_in, preferred_element_type=jnp.float32)
    hidden = exact_gelu(pre).astype(jnp.bfloat16)
    ff_out = jnp.dot(hidden, full_down, preferred_element_type=jnp.float32)
    result, scaled_two, inv_two = normalize(first + ff_out, gain_two, bias_two)
    upstream = cotangent[0].astype(jnp.float32)
    grad_two, grad_gain_two, grad_bias_two = normalize_back(upstream, scaled_two, inv_two, gain_two)
    ff_grad = grad_two.astype(jnp.bfloat16)
    grad_down = jnp.einsum("tf,td->fd", hidden, ff_grad, preferred_element_type=jnp.float32)
    hidden_grad = jnp.einsum("td,fd->tf", ff_grad, full_down, preferred_element_type=jnp.float32)
    gelu_pull = jax.vjp(exact_gelu, pre)[1]
    pre_grad = gelu_pull(hidden_grad)[0].astype(jnp.bfloat16)
    grad_in = jnp.einsum("td,tf->df", first_low, pre_grad, preferred_element_type=jnp.float32)
    first_grad = grad_two + jnp.einsum(
        "tf,df->td", pre_grad, full_in, preferred_element_type=jnp.float32
    )
    grad_one, grad_gain_one, grad_bias_one = normalize_back(
        first_grad, scaled_one, inv_one, gain_one
    )
    attn_grad = grad_one.astype(jnp.bfloat16)
    grad_out_weight = jnp.einsum("tc,td->cd", mixed, attn_grad, preferred_element_type=jnp.float32)
    mixed_grad = jnp.einsum(
        "td,cd->tc", attn_grad, full_out, preferred_element_type=jnp.float32
    ).astype(jnp.bfloat16)
    grad_blocks = lax.all_to_all(
        mixed_grad.reshape(tok_rows, groups, group_width),
        "aa",
        split_axis=1,
        concat_axis=0,
        tiled=True,
    )
    grad_blocks = grad_blocks.reshape(block_count, QBLK, head_local, HEAD)
    delta = jnp.transpose(jnp.sum(grad_blocks.astype(jnp.float32) * attn_heads, axis=-1), (0, 2, 1))
    grad_pair = jnp.zeros((block_len, 2, head_local, HEAD), jnp.float32)
    query_grad = jnp.zeros((block_count, QBLK, head_local, HEAD), jnp.float32)
    for cycle_step in range(cycle_size):
        if cycle_step > 0:
            grad_pair = pass_grads(grad_pair)
        key_start = (cycle_index - cycle_step) % cycle_size * block_len
        current_pair = kept_pairs[cycle_step]
        key_heads = current_pair[:, 0]
        value_heads = current_pair[:, 1]

        def visit(carry, inputs):
            block_index, query_block, grad_block, log_block, delta_block = inputs
            allowed = allowed_mask(
                seq_segments, seq_valid, query_base + block_index * QBLK, key_start, QBLK, block_len
            )
            scores = (
                jnp.einsum(
                    "qhd,khd->hqk", query_block, key_heads, preferred_element_type=jnp.float32
                )
                * score_scale
            )
            scores = jnp.where(allowed[None], scores, MASKED_SCORE)
            probs = jnp.exp(scores - log_block[..., None])
            value_part = jnp.einsum(
                "hqk,qhd->khd",
                probs.astype(jnp.bfloat16),
                grad_block,
                preferred_element_type=jnp.float32,
            )
            prob_grad = jnp.einsum(
                "qhd,khd->hqk", grad_block, value_heads, preferred_element_type=jnp.float32
            )
            score_grad = (probs * (prob_grad - delta_block[..., None])).astype(jnp.bfloat16)
            query_part = (
                jnp.einsum(
                    "hqk,khd->qhd", score_grad, key_heads, preferred_element_type=jnp.float32
                )
                * score_scale
            )
            key_part = (
                jnp.einsum(
                    "hqk,qhd->khd", score_grad, query_block, preferred_element_type=jnp.float32
                )
                * score_scale
            )
            return (carry + jnp.stack([key_part, value_part], axis=1), query_part)

        grad_pair, query_part = lax.scan(
            visit, grad_pair, (block_ids, q_blocks, grad_blocks, log_total, delta)
        )
        query_grad = query_grad + query_part
    grad_pair = pass_grads(grad_pair)
    head_grads = jnp.concatenate(
        [query_grad.reshape(block_len, 1, head_local, HEAD), grad_pair], axis=1
    ).astype(jnp.bfloat16)
    token_grads = lax.all_to_all(
        head_grads.reshape(block_len, 1, 3 * group_width),
        "aa",
        split_axis=0,
        concat_axis=1,
        tiled=True,
    )
    token_grads = token_grads.reshape(tok_rows, groups, 3, group_width)
    query_tok = token_grads[:, :, 0].reshape(tok_rows, width)
    key_tok = token_grads[:, :, 1].reshape(tok_rows, width)
    value_tok = token_grads[:, :, 2].reshape(tok_rows, width)
    input_grad = grad_one
    input_grad = input_grad + jnp.einsum(
        "td,cd->tc", query_tok, full_query, preferred_element_type=jnp.float32
    )
    input_grad = input_grad + jnp.einsum(
        "td,cd->tc", key_tok, full_key, preferred_element_type=jnp.float32
    )
    input_grad = input_grad + jnp.einsum(
        "td,cd->tc", value_tok, full_value, preferred_element_type=jnp.float32
    )
    weight_grads = (
        jnp.einsum("tc,td->cd", token_rows, query_tok, preferred_element_type=jnp.float32),
        jnp.einsum("tc,td->cd", token_rows, key_tok, preferred_element_type=jnp.float32),
        jnp.einsum("tc,td->cd", token_rows, value_tok, preferred_element_type=jnp.float32),
        grad_out_weight,
        grad_gain_one,
        grad_bias_one,
        grad_in,
        grad_down,
        grad_gain_two,
        grad_bias_two,
    )
    halves = (
        *tuple(
            (
                part.astype(jnp.float32)
                for part in side_by_side(
                    (
                        weight_grads[0].astype(jnp.bfloat16),
                        weight_grads[1].astype(jnp.bfloat16),
                        weight_grads[2].astype(jnp.bfloat16),
                        weight_grads[3].astype(jnp.bfloat16),
                        weight_grads[4].astype(jnp.bfloat16),
                        weight_grads[5].astype(jnp.bfloat16),
                        weight_grads[6].astype(jnp.bfloat16),
                    ),
                    "shard",
                    0,
                    1,
                )
            )
        ),
        lax.psum_scatter(
            weight_grads[7].astype(jnp.bfloat16), "shard", scatter_dimension=0, tiled=True
        ).astype(jnp.float32),
        lax.psum_scatter(
            weight_grads[8].astype(jnp.bfloat16), "shard", scatter_dimension=0, tiled=True
        ).astype(jnp.float32),
        lax.psum_scatter(
            weight_grads[9].astype(jnp.bfloat16), "shard", scatter_dimension=0, tiled=True
        ).astype(jnp.float32),
    )
    pieces = one_scatter(
        (
            halves[0],
            halves[1],
            halves[2],
            halves[3],
            halves[4],
            halves[5],
            halves[6],
            halves[7],
            halves[8],
            halves[9],
        ),
        ("blk", "aa"),
        (0, 0, 0, 0, 0, 0, 0, 0, 0, 0),
    )
    shares = (
        *tuple(
            (
                part.astype(jnp.float32)
                for part in sent_together(
                    (
                        pieces[0].astype(jnp.bfloat16),
                        pieces[1].astype(jnp.bfloat16),
                        pieces[2].astype(jnp.bfloat16),
                        pieces[3].astype(jnp.bfloat16),
                        pieces[4].astype(jnp.bfloat16),
                        pieces[5].astype(jnp.bfloat16),
                        pieces[6].astype(jnp.bfloat16),
                    ),
                    ("blk", "aa"),
                    0,
                    1,
                )
            )
        ),
        lax.all_gather(pieces[7].astype(jnp.bfloat16), ("blk", "aa"), axis=0, tiled=True).astype(
            jnp.float32
        ),
        lax.all_gather(pieces[8].astype(jnp.bfloat16), ("blk", "aa"), axis=0, tiled=True).astype(
            jnp.float32
        ),
        lax.all_gather(pieces[9].astype(jnp.bfloat16), ("blk", "aa"), axis=0, tiled=True).astype(
            jnp.float32
        ),
    )
    return (
        result.astype(jnp.bfloat16)[None],
        input_grad.astype(jnp.bfloat16)[None],
        shares[0],
        shares[1],
        shares[2],
        shares[3],
        shares[4],
        shares[5],
        shares[6],
        shares[7],
        shares[8],
        shares[9],
    )


def solution(mesh):
    return jax.shard_map(
        shards,
        mesh=mesh,
        in_specs=(
            P("shard", ("blk", "aa"), None),
            P("shard", None),
            P("shard", None),
            P("shard", None),
            P("shard", None),
            P("shard", None),
            P("shard", None),
            P("shard"),
            P("shard"),
            P("shard", None),
            P("shard", None),
            P("shard"),
            P("shard"),
            P("shard", ("blk", "aa"), None),
        ),
        out_specs=(
            P("shard", ("blk", "aa"), None),
            P("shard", ("blk", "aa"), None),
            P("shard", None),
            P("shard", None),
            P("shard", None),
            P("shard", None),
            P("shard"),
            P("shard"),
            P("shard", None),
            P("shard", None),
            P("shard"),
            P("shard"),
        ),
        check_vma=False,
    )
```

profile of v0, /device:TPU:1, one launch (start us, length us, event | category | flops | bytes accessed | tf_op | source)
XLA Modules:
  0.0 1731.6 jit_solution(8989298247558518679)
XLA Ops:
  8.9 16.6 concatenate.24
  25.5 211.6 %all-gather.7.cloned.1.call-done = bf16[1024,8194]{1,0:T(8,128)(2,1)} async-done(((bf16[512,8194]{1,0:T(8,128)(2,1)}), bf16[1024,8194]{1,0:T(8,128)(2,1)}) %all-gather.7.cloned.1.call-update) | async-done | bytes 16781328 | tf_op jit(solution)/shard_map/all_gather | solution.py:27
  252.7 12.3 all-to-all-done
  269.5 22.4 %while.121 = (s32[]{:T(128)}, f32[4,1,512]{2,1,0:T(1,128)S(1)}, f32[4,1,512]{2,1,0:T(1,128)S(1)}, f32[4,512,1,64]{1,3,2,0:T(8,128)S(1)}, s32[4]{0:T(128)S(1)}, /...) while((s32[]{:T(128)}, f32[4,1,512]{2,1,0:T(1,128)S(1)}, ...), condition=%wide.region_3.4_spmd, body=%wide.region_0.3_spmd.sunk | while | flops 280009216 | bytes 13375747 | solution.py:208
  292.2 18.8 %while.122 = (s32[]{:T(128)}, f32[4,1,512]{2,1,0:T(1,128)S(1)}, f32[4,1,512]{2,1,0:T(1,128)S(1)}, f32[4,512,1,64]{1,3,2,0:T(8,128)S(1)}, f32[4,1,512]{2,1,0:T(1,...) while((s32[]{:T(128)}, f32[4,1,512]{2,1,0:T(1,128)S(1)}, ...), condition=%wide.region_7.8_spmd, body=%wide.region_4.7_spmd.sunk | while | flops 280042496 | bytes 13519135 | solution.py:208
  315.3 18.7 %while.123 = (s32[]{:T(128)}, f32[4,1,512]{2,1,0:T(1,128)S(1)}, f32[4,1,512]{2,1,0:T(1,128)S(1)}, f32[4,512,1,64]{1,3,2,0:T(8,128)S(1)}, f32[4,1,512]{2,1,0:T(1,...) while((s32[]{:T(128)}, f32[4,1,512]{2,1,0:T(1,128)S(1)}, ...), condition=%wide.region_11.12_spmd, body=%wide.region_8.11_spmd.sunk | while | flops 280042496 | bytes 13519135 | solution.py:208
  336.0 33.8 %while.124 = (s32[]{:T(128)}, f32[4,1,512]{2,1,0:T(1,128)S(1)}, f32[4,1,512]{2,1,0:T(1,128)S(1)}, f32[4,512,1,64]{1,0,3,2:T(4,128)}, f32[4,1,512]{2,1,0:T(1,128)...) while((s32[]{:T(128)}, f32[4,1,512]{2,1,0:T(1,128)S(1)}, ...), condition=%wide.region_15.16_spmd, body=%wide.region_12.15_spmd.sunk | while | flops 280042496 | bytes 14043427 | solution.py:208
  392.6 19.3 %multiply_convert_fusion.4 = (bf16[128,4096]{1,0:T(8,128)(2,1)S(1)}, f32[128,4096]{1,0:T(8,128)}) fusion(bf16[1024,8194]{1,0:T(8,128)(2,1)} %all-gather.7.cloned.1.call-done, f32[128,1024]{1,0:T(8,128)S(1)} %get-tuple-element.2492, f32[1024]{0:T(1024)S(1)} %get-tuple-element.2162, f32[1024]{0:T(1024)S(1)} %get-tuple-element.2161, ...), kind=kOutput, calls=%fused_computation.224 | convolution fusion | flops 1108475904 | bytes 12067840 | tf_op jit(solution)/shard_map/dot_general | solution.py:224
  448.3 45.7 %while.128 = (s32[]{:T(128)}, f32[2048,2,1,64]{0,3,2,1:T(8,128)}, f32[4,512,1,64]{1,3,2,0:T(8,128)}, bf16[4,512,1,64]{1,3,2,0:T(8,128)(2,1)S(1)}, s32[4]{0:T(128...) while((s32[]{:T(128)}, f32[2048,2,1,64]{0,3,2,1:T(8,128)}, ...), condition=%wide.region_26.27_spmd.clone, body=%wide.region_25.26_spmd.clone.sunk | while | flops 683577856 | bytes 28502424 | solution.py:303
  507.1 26.6 %while.125 = (s32[]{:T(128)}, f32[2048,2,1,64]{0,3,2,1:T(8,128)S(1)}, f32[4,512,1,64]{1,3,2,0:T(8,128)}, bf16[4,512,1,64]{1,3,2,0:T(8,128)(2,1)S(1)}, s32[4]{0:T...) while((s32[]{:T(128)}, ...), condition=%wide.region_28.29_spmd, body=%wide.region_27.28_spmd.sunk | while | flops 683315712 | bytes 24308000 | solution.py:303
  545.2 24.1 %while.126 = (s32[]{:T(128)}, f32[2048,2,1,64]{0,3,2,1:T(8,128)S(1)}, f32[4,512,1,64]{1,3,2,0:T(8,128)S(1)}, bf16[4,512,1,64]{1,3,2,0:T(8,128)(2,1)S(1)}, s32[4]...) while((s32[]{:T(128)}, ...), condition=%wide.region_30.31_spmd, body=%wide.region_29.30_spmd.sunk | while | flops 683315712 | bytes 24308000 | solution.py:303
  572.0 17.3 %collective-permute-done.5 = bf16[2048,2,1,64]{0,3,2,1:T(8,128)(2,1)} collective-permute-done((bf16[2048,2,1,64]{0,3,2,1:T(8,128)(2,1)S(1)}, bf16[2048,2,1,64]{0,3,2,1:T(8,128)(2,1)}, u32[]{:S(2)}, u32[]{:S(2)}) %collective-permute-start.5) | collective-permute-done | bytes 524320 | tf_op jit(solution)/shard_map/ppermute | solution.py:19
  590.6 24.1 %while.127 = (s32[]{:T(128)}, f32[2048,2,1,64]{0,3,2,1:T(8,128)S(1)}, f32[4,512,1,64]{1,3,2,0:T(8,128)S(1)}, bf16[4,512,1,64]{1,3,2,0:T(8,128)(2,1)S(1)}, s32[4]...) while((s32[]{:T(128)}, ...), condition=%wide.region_32.33_spmd, body=%wide.region_31.32_spmd.sunk | while | flops 683315712 | bytes 24308000 | solution.py:303
  619.4 15.6 collective-permute-done.6
  689.2 31.0 %concatenate.28 = bf16[1024,8194]{1,0:T(8,128)(2,1)} concatenate(bf16[1024,1024]{1,0:T(8,128)(2,1)} %copy.197, bf16[1024,1024]{1,0:T(8,128)(2,1)} %copy.198, bf16[1024,1024]{1,0:T(8,128)(2,1)} %copy.199, bf16[1024,1024]{1,0:T(8,128)(2,1)S(1)} %copy.200, bf16[1024,1]{1,0:T(8,128)(2,1)S(1)} %copy-done.37, bf16[1024,1]{1,0:T(8,128)(2,1)S(1)} %copy-done.38, ...), dimensions={1} | concatenate | bytes 33562624 | tf_op jit(solution)/shard_map/concatenate | solution.py:36
  735.8 181.8 %reduce-scatter.7.cloned.1.call-done = bf16[512,8194]{1,0:T(8,128)(2,1)} async-done(((bf16[1024,8194]{1,0:T(8,128)(2,1)}), bf16[512,8194]{1,0:T(8,128)(2,1)}) %reduce-scatter.7.cloned.1.call-update) | async-done | bytes 8390672 | tf_op jit(solution)/shard_map/reduce_scatter | solution.py:37
  950.5 27.3 %dynamic-update-slice.8 = bf16[64,98336]{1,0:T(8,128)(2,1)} dynamic-update-slice(bf16[64,98336]{1,0:T(8,128)(2,1)} %dynamic-update-slice.7, bf16[64,32768]{1,0:T(8,128)(2,1)} %reshape_reshape.28, s32[]{} %constant.542, s32[]{} %constant.548) | dynamic-update-slice | bytes 8388612
  977.9 26.8 %dynamic-update-slice.9 = bf16[64,98336]{1,0:T(8,128)(2,1)} dynamic-update-slice(bf16[64,98336]{1,0:T(8,128)(2,1)} %dynamic-update-slice.8, bf16[64,32768]{1,0:T(8,128)(2,1)} %reshape_reshape.29, s32[]{} %constant.542, s32[]{} %constant.549) | dynamic-update-slice | bytes 8388612
  1007.6 14.2 pad_convert_fusion
  1021.7 19.2 %reshape.1136 = f32[49664,128]{1,0:T(8,128)} reshape(f32[64,99328]{1,0:T(8,128)} %pad_convert_fusion) | data formatting | bytes 50855936 | tf_op jit(solution)/shard_map/reshape | solution.py:55
  1041.1 334.9 %reduce-scatter.11.cloned.1.call-done = f32[776,128]{1,0:T(8,128)} async-done(((f32[49664,128]{1,0:T(8,128)}), f32[776,128]{1,0:T(8,128)}) %reduce-scatter.11.cloned.1.call-update) | async-done | bytes 397328
  1389.8 129.8 %all-reduce.6 = (bf16[512]{0:T(512)(128)(2,1)S(1)}, bf16[512]{0:T(512)(128)(2,1)S(1)}) all-reduce(bf16[512]{0:T(512)(128)(2,1)S(1)} %dynamic-update-slice, bf16[512]{0:T(512)(128)(2,1)S(1)} %dynamic-update-slice.1), channel_id=1, replica_groups=mesh['shard'=2,'blk'=4,'aa'=16] {'blk','aa'}, use_global_device_ids=true, to_apply=%add.1 | all-reduce | flops 1024 | bytes 4096
  1520.8 19.6 %all-gather.13.cloned.1.call-done = bf16[2048,1024]{1,0:T(8,128)(2,1)} async-done(((bf16[32,1024]{1,0:T(8,128)(2,1)}), bf16[2048,1024]{1,0:T(8,128)(2,1)}) %all-gather.13.cloned.1.call-update) | async-done | bytes 4194320 | tf_op jit(solution)/shard_map/all_gather | solution.py:410
  1547.0 163.2 %all-gather.11.cloned.1.call-done = bf16[512,8194]{1,0:T(8,128)(2,1)} async-done(((bf16[8,8194]{1,0:T(8,128)(2,1)}), bf16[512,8194]{1,0:T(8,128)(2,1)}) %all-gather.11.cloned.1.call-update) | async-done | bytes 8390672 | tf_op jit(solution)/shard_map/all_gather | solution.py:27
  (750 shorter events, 450.5 us)
Async XLA Ops:
  7.2 229.9 %all-gather.7.cloned.1.call-start = ((), (), s32[]{:S(2)}) async-start(), calls=%async_computation.7 | async-start | bytes 25559040 | tf_op jit(solution)/shard_map/all_gather | solution.py:27
  25.5 211.6 %copy-start.27 = (bf16[1,128,1024]{2,1,0:T(8,128)(2,1)S(1)}, bf16[1,128,1024]{2,1,0:T(8,128)(2,1)}, u32[]{:S(2)}) copy-start(bf16[1,128,1024]{2,1,0:T(8,128)(2,1)} %param.30) | copy-start | bytes 786436
  245.1 19.9 %all-to-all-start = ((bf16[128,16,192]{0,2,1:T(8,128)(2,1)}), bf16[128,16,192]{0,2,1:T(8,128)(2,1)S(1)}, u32[]{:S(2)}, u32[]{:S(2)}) async-start(bf16[128,16,192]{0,2,1:T(8,128)(2,1)} %pad_maximum_fusion), calls=%async_computation | async-start | bytes 1572864 | tf_op jit(solution)/shard_map/all_to_all | solution.py:161
  251.8 160.1 %all-gather.9.cloned.1.call-start = ((), (), s32[]{:S(2)}) async-start(), calls=%async_computation.8 | async-start | bytes 12582912 | tf_op jit(solution)/shard_map/all_gather | solution.py:121
  266.9 25.0 %collective-permute-start = (bf16[2048,2,1,64]{0,3,1,2:T(8,128)(2,1)S(1)}, bf16[2048,2,1,64]{0,3,1,2:T(8,128)(2,1)S(1)}, u32[]{:S(2)}, u32[]{:S(2)}) collective-permute-start(bf16[2048,2,1,64]{0,3,1,2:T(8,128)(2,1)S(1)} %slice.147), channel_id=1, source_target_pairs={{0,16},{16,32},{32,48},{48,0},{1,17},{17,33},{33,49},{49,1},{2,18}... | collective-permute-start | bytes 1572872 | tf_op jit(solution)/shard_map/ppermute | solution.py:19
  292.0 20.4 %collective-permute-start.1 = (bf16[2048,2,1,64]{0,3,1,2:T(8,128)(2,1)S(1)}, bf16[2048,2,1,64]{0,3,1,2:T(8,128)(2,1)}, u32[]{:S(2)}, u32[]{:S(2)}) collective-permute-start(bf16[2048,2,1,64]{0,3,1,2:T(8,128)(2,1)S(1)} %collective-permute-done), channel_id=1, source_target_pairs={{0,16},{16,32},{32,48},{48,0},{1,17},{17,33},{33,49},{49,1},{2,18}... | collective-permute-start | bytes 1572872 | tf_op jit(solution)/shard_map/ppermute | solution.py:19
  313.4 21.4 %collective-permute-start.2 = (bf16[2048,2,1,64]{0,3,1,2:T(8,128)(2,1)}, bf16[2048,2,1,64]{0,3,1,2:T(8,128)(2,1)}, u32[]{:S(2)}, u32[]{:S(2)}) collective-permute-start(bf16[2048,2,1,64]{0,3,1,2:T(8,128)(2,1)} %collective-permute-done.1), channel_id=1, source_target_pairs={{0,16},{16,32},{32,48},{48,0},{1,17},{17,33},{33,49},{49,1},{2,18}... | collective-permute-start | bytes 1572872 | tf_op jit(solution)/shard_map/ppermute | solution.py:19
  374.1 14.6 all-to-all-start.1
  388.7 42.1 %copy-start.49 = (f32[1024]{0:T(1024)}, f32[1024]{0:T(1024)S(1)}, u32[]{:S(2)}) copy-start(f32[1024]{0:T(1024)S(1)} %get-tuple-element.2161) | copy-start | bytes 12292
  392.3 38.5 %copy-start.9 = (f32[128,1024]{1,0:T(8,128)}, f32[128,1024]{1,0:T(8,128)S(1)}, u32[]{:S(2)}) copy-start(f32[128,1024]{1,0:T(8,128)S(1)} %get-tuple-element.2492) | copy-start | bytes 1572868
  392.3 38.5 %copy-start.54 = (f32[128]{0:T(128)}, f32[128]{0:T(128)S(1)}, u32[]{:S(2)}) copy-start(f32[128]{0:T(128)S(1)} %broadcast_multiply_fusion.5) | copy-start | bytes 1540
  433.0 13.9 all-to-all-start.2
  439.4 289.0 %reduce-scatter.9.cloned.1.call-start = ((), (), s32[]{:S(2)}) async-start(), calls=%async_computation.10 | async-start | bytes 12582912 | tf_op jit(solution)/shard_map/reduce_scatter | solution.py:364
  495.4 10.7 collective-permute-start.3
  534.6 9.3 collective-permute-start.4
  569.4 19.9 %collective-permute-start.5 = (bf16[2048,2,1,64]{0,3,2,1:T(8,128)(2,1)S(1)}, bf16[2048,2,1,64]{0,3,2,1:T(8,128)(2,1)}, u32[]{:S(2)}, u32[]{:S(2)}) collective-permute-start(bf16[2048,2,1,64]{0,3,2,1:T(8,128)(2,1)S(1)} %convert_element_type.367), channel_id=1, source_target_pairs={{0,16},{16,32},{32,48},{48,0},{1,17},{17,33},{33,49},{49,1},{2,18}... | collective-permute-start | bytes 1572872 | tf_op jit(solution)/shard_map/ppermute | solution.py:19
  614.8 20.2 %collective-permute-start.6 = (bf16[2048,2,1,64]{0,3,1,2:T(8,128)(2,1)S(1)}, bf16[2048,2,1,64]{0,3,1,2:T(8,128)(2,1)S(1)}, u32[]{:S(2)}, u32[]{:S(2)}) collective-permute-start(bf16[2048,2,1,64]{0,3,1,2:T(8,128)(2,1)S(1)} %bitcast_convert_fusion), channel_id=1, source_target_pairs={{0,16},{16,32},{32,48},{48,0},{1,17},{17,33},{33,49},{49,1},{2,18}... | collective-permute-start | bytes 1572872 | tf_op jit(solution)/shard_map/ppermute | solution.py:19
  638.9 18.4 %all-to-all-start.3 = ((bf16[16,2,12288]{2,1,0:T(2,128)(2,1)}), bf16[16,2,12288]{2,1,0:T(2,128)(2,1)}, u32[]{:S(2)}, u32[]{:S(2)}) async-start(bf16[16,2,12288]{2,1,0:T(2,128)(2,1)} %reshape.1174), calls=%async_computation.3 | async-start | bytes 1572864 | tf_op jit(solution)/shard_map/all_to_all | solution.py:311
  643.2 274.4 %reduce-scatter.7.cloned.1.call-start = ((), (), s32[]{:S(2)}) async-start(), calls=%async_computation.9 | async-start | bytes 25559040 | tf_op jit(solution)/shard_map/reduce_scatter | solution.py:37
  720.3 655.7 %reduce-scatter.11.cloned.1.call-start = ((), (), s32[]{:S(2)}) async-start(), calls=%async_computation.13 | async-start | bytes 25825280
  1041.0 339.1 %copy-start.67 = (u32[128]{0:T(128)S(1)}, u32[128]{0:T(128)}, u32[]{:S(2)}) copy-start(u32[128]{0:T(128)} %constant.510) | copy-start | bytes 1540
  1041.0 340.4 %copy-start.43 = (bf16[128,16,1,64]{0,3,2,1:T(8,128)(2,1)S(1)}, bf16[128,16,1,64]{0,3,2,1:T(8,128)(2,1)}, u32[]{:S(2)}) copy-start(bf16[128,16,1,64]{0,3,2,1:T(8,128)(2,1)} %get-tuple-element.2461) | copy-start | bytes 786436
  1041.0 499.3 %all-gather.13.cloned.1.call-start = ((), (), s32[]{:S(2)}) async-start(), calls=%async_computation.12 | async-start | bytes 4259840 | tf_op jit(solution)/shard_map/all_gather | solution.py:410
  1377.8 332.4 %all-gather.11.cloned.1.call-start = ((), (), s32[]{:S(2)}) async-start(), calls=%async_computation.11 | async-start | bytes 8652800 | tf_op jit(solution)/shard_map/all_gather | solution.py:27
  (81 other events, 657.8 us)
Sparse Core Ops, SparseCore 0:
  25.6 211.4 all-gather.6
  254.3 124.9 all-gather.8
  543.6 109.5 reduce-scatter.8
  720.4 197.1 reduce-scatter.6
  1041.1 334.8 reduce-scatter.10
  1378.1 162.2 all-gather.12
  1542.6 167.5 all-gather.10
where the time goes:
time: 1750 us; the launch traced here: 1730 us
  waiting for transfers between devices  971 us (55%)
  local copies, waits for them, and re-layouts  255 us (15%)
  matrix products  206 us (12%)
  blocking collectives  145 us (8%)
  other arithmetic  75.3 us (4%)
  starting transfers between devices  38.5 us (2%)
  loops' own time  23.1 us (1%)
    all_gather x2, waiting for transfers between devices, sent_together(): filled = lax.all_gather(both, axis, axis=dim, tiled=True)  375 us
    unnamed x8, waiting for transfers between devices  336 us
    reduce_scatter x1, waiting for transfers between devices, side_by_side(): lax.psum_scatter(both, axis, scatter_dimension=dim, tiled=True)  182 us
    unnamed x2, blocking collectives  135 us
    unnamed x171, local copies, waits for them, and re-layouts  80.6 us
    ppermute x7, waiting for transfers between devices, from_behind(): lax.ppermute(value, axis, [(i, (i + by) % devices) for i in range(devices)])  39.5 us
  transfers between devices with their start and end apart: 18, of which 11 were waited for; matrix products, arithmetic and copies ran while one was open for 16% of the time, Pallas kernels for 0%

commit v1 on v0

--- a/solution.py
+++ b/solution.py
@@ -1,8 +1,11 @@
+import functools
 import math
 
 import jax
 import jax.numpy as jnp
 from jax import lax
+from jax.experimental import pallas as pl
+from jax.experimental.pallas import tpu as pltpu
 from jax.sharding import PartitionSpec as P
 
 HEADS = 16
@@ -19,46 +22,449 @@
     return lax.ppermute(value, axis, [(i, (i + by) % devices) for i in range(devices)])
 
 
-def sent_together(arrays, axis, dim, along):
-    widths = [math.prod(a.shape[along:]) for a in arrays]
-    both = jnp.concatenate(
-        [a.reshape(*a.shape[:along], w) for a, w in zip(arrays, widths)], axis=along
-    )
-    filled = lax.all_gather(both, axis, axis=dim, tiled=True)
-    pieces = jnp.split(filled, [sum(widths[:k]) for k in range(1, len(widths))], axis=along)
-    return tuple(
-        (b.reshape(*filled.shape[:along], *a.shape[along:]) for a, b in zip(arrays, pieces))
-    )
-
-
-def side_by_side(arrays, axis, dim, along):
-    columns = [a.reshape(*a.shape[:along], -1) for a in arrays]
-    both = jnp.concatenate(columns, axis=along)
-    filled, at, gathered = (lax.psum_scatter(both, axis, scatter_dimension=dim, tiled=True), 0, [])
-    for a, column in zip(arrays, columns):
-        piece = filled[..., at : at + column.shape[along]]
-        gathered.append(piece.reshape(*piece.shape[:along], *a.shape[along:]))
-        at += column.shape[along]
-    return tuple(gathered)
-
-
-def split_up(value, dim, devices):
-    before, after = (value.shape[:dim], value.shape[dim + 1 :])
-    return jnp.moveaxis(value.reshape(*before, devices, -1, *after), dim, 0)
-
-
-def one_scatter(arrays, axis, dims):
-    devices = lax.axis_size(axis)
-    pieces = [split_up(a, dim, devices) for a, dim in zip(arrays, dims)]
-    lines = jnp.concatenate([b.reshape(devices, -1) for b in pieces], axis=1)
-    span = max(16, -(-lines.shape[1] // 1024) * 8)
-    lines = jnp.pad(lines, ((0, 0), (0, span * 128 - lines.shape[1]))).reshape(-1, 128)
-    flat, at, gathered = (lax.psum_scatter(lines, axis, tiled=True).reshape(-1), 0, [])
-    for b in pieces:
-        part = b[0]
-        gathered.append(flat[at : at + part.size].reshape(part.shape))
-        at += part.size
-    return tuple(gathered)
+MESH = pl.DeviceIdType.MESH
+ROWS = 512
+REDUCE_DIMS = ("xa", "ya", "za", "yb", "zb")
+GATHER_DIMS = ("ya", "za", "yb", "zb")
+
+
+def place():
+    shard = lax.axis_index("shard")
+    blk = lax.axis_index("blk")
+    aa = lax.axis_index("aa")
+    return (shard, blk // 2, blk % 2, aa // 4, aa % 4)
+
+
+def flipped(i):
+    return i + 1 - 2 * (i % 2)
+
+
+def partner(dim):
+    shard, x_lo, core, z, y = place()
+    if dim == "core":
+        core = 1 - core
+    elif dim == "xa":
+        x_lo = 1 - x_lo
+    elif dim == "xb":
+        shard, x_lo = 1 - shard, 1 - x_lo
+    elif dim == "ya":
+        y = flipped(y)
+    elif dim == "yb":
+        y = 3 - y
+    elif dim == "za":
+        z = flipped(z)
+    else:
+        z = 3 - z
+    return (shard, x_lo * 2 + core, z * 4 + y)
+
+
+def ring_bit(dim):
+    shard, x_lo, _, z, y = place()
+    if dim == "xa":
+        return (shard * 2 + x_lo + shard) % 2
+    if dim == "ya":
+        return (y + y // 2) % 2
+    if dim == "yb":
+        return y // 2
+    if dim == "za":
+        return (z + z // 2) % 2
+    return z // 2
+
+
+def greet(dims):
+    barrier = pltpu.get_barrier_semaphore()
+    for dim in dims:
+        pl.semaphore_signal(barrier, inc=1, device_id=partner(dim), device_id_type=MESH)
+    pl.semaphore_wait(barrier, len(dims))
+
+
+def remote(src, dst, send_sem, recv_sem, dim):
+    return pltpu.make_async_remote_copy(
+        src_ref=src,
+        dst_ref=dst,
+        send_sem=send_sem,
+        recv_sem=recv_sem,
+        device_id=partner(dim),
+        device_id_type=MESH,
+    )
+
+
+def row_starts(dims, rows):
+    starts, at, size = ([0], 0, rows)
+    for dim in dims:
+        size //= 2
+        at = at + ring_bit(dim) * size
+        starts.append(at)
+    return starts
+
+
+def rotated(dims, by):
+    return dims[by:] + dims[:by]
+
+
+def gather_kernel(shapes, targets, n_out, *refs):
+    n = len(shapes)
+    ins, outs = (refs[:n], refs[n : n + n_out])
+    send, recv, own = refs[n + n_out :]
+    shard, _, core, _, _ = place()
+    greet(("xb", "core") + GATHER_DIMS)
+    sent = []
+
+    def start(copy):
+        copy.start()
+        sent.append(copy)
+
+    locals_ = []
+    for i, (rows, cols) in enumerate(shapes):
+        out, off = targets[i]
+        copy = pltpu.make_async_copy(
+            ins[i],
+            outs[out].at[pl.ds(pl.multiple_of(shard * rows, rows), rows), pl.ds(off, cols)],
+            own.at[i],
+        )
+        copy.start()
+        locals_.append(copy)
+
+    def block(i, part, base, at, size, inner=False):
+        rows, cols = shapes[i]
+        out, off = targets[i]
+        width = cols // 8
+        col = pl.multiple_of(core * (cols // 2) + part * width, 128)
+        if inner:
+            return ins[i].at[pl.ds(pl.multiple_of(at, 16), size), pl.ds(col, width)]
+        col = pl.multiple_of(core * (cols // 2) + (off + part * width), 128)
+        at = pl.multiple_of(base * rows + at, 16)
+        return outs[out].at[pl.ds(at, size), pl.ds(col, width)]
+
+    other = 1 - shard
+    plan = {}
+    for i, (rows, _) in enumerate(shapes):
+        for part in range(4):
+            order = rotated(GATHER_DIMS, part)
+            starts = row_starts(order, rows)
+            piece = rows // 16
+            copy = remote(
+                block(i, part, 0, starts[4], piece, inner=True),
+                block(i, part, shard, starts[4], piece),
+                send.at[i, part, 0],
+                recv.at[i, part, 0],
+                "xb",
+            )
+            start(copy)
+            plan[i, part] = (order, starts, copy)
+    siblings = []
+    for stage in range(1, 6):
+        for i, (rows, _) in enumerate(shapes):
+            for part in range(4):
+                order, starts, copy = plan[i, part]
+                copy.wait_recv()
+                if stage < 5:
+                    k = 4 - stage
+                    size = rows >> (k + 1)
+                    mine = block(i, part, other, starts[k + 1], size)
+                    copy = remote(
+                        mine, mine, send.at[i, part, stage], recv.at[i, part, stage], order[k]
+                    )
+                    start(copy)
+                    plan[i, part] = (order, starts, copy)
+                if stage >= 4:
+                    size = rows // 2
+                    at = starts[1] if stage == 4 else size - starts[1]
+                    mine = block(i, part, other, at, size)
+                    copy = remote(
+                        mine, mine, send.at[i, part, stage + 1], recv.at[i, part, stage + 1], "core"
+                    )
+                    start(copy)
+                    siblings.append(copy)
+    for copy in siblings:
+        copy.wait_recv()
+    for copy in sent:
+        copy.wait_send()
+    for copy in locals_:
+        copy.wait()
+
+
+def gather_weights(arrays, targets, out_shapes, collective_id):
+    shapes = [a.shape for a in arrays]
+    n = len(shapes)
+    return pl.pallas_call(
+        functools.partial(gather_kernel, shapes, targets, len(out_shapes)),
+        out_shape=[jax.ShapeDtypeStruct(shape, jnp.bfloat16) for shape in out_shapes],
+        in_specs=[pl.BlockSpec(memory_space=pl.ANY)] * n,
+        out_specs=[pl.BlockSpec(memory_space=pl.ANY)] * len(out_shapes),
+        scratch_shapes=[
+            pltpu.SemaphoreType.DMA((n, 4, 7)),
+            pltpu.SemaphoreType.DMA((n, 4, 7)),
+            pltpu.SemaphoreType.DMA((n,)),
+        ],
+        compiler_params=pltpu.CompilerParams(collective_id=collective_id, has_side_effects=True),
+    )(*arrays)
+
+
+def reduce_kernel(n_left, dots, widths, with_norm, *refs):
+    refs = list(refs)
+
+    def take(count):
+        taken = refs[:count]
+        del refs[:count]
+        return taken
+
+    n_right = len(dots_rights(dots))
+    lefts, rights = (take(n_left), take(n_right))
+    norm_in = take(1)[0] if with_norm else None
+    out = take(1)[0]
+    norm_out = take(1)[0] if with_norm else None
+    left_all, right_all = (take(n_left), take(n_right))
+    partial = take(1)[0]
+    landed = take(6)
+    norm_held, norm_landed = take(2) if with_norm else (None, None)
+    act_send, act_recv, red_send, red_recv, gat_send, gat_recv, nrm_send, nrm_recv = refs
+    shard, _, core, _, _ = place()
+    greet(("core", "xa", "xb", "ya", "yb", "za", "zb"))
+    sent = []
+
+    def start(copy):
+        copy.start()
+        sent.append(copy)
+        return copy
+
+    half_tokens = lefts[0].shape[0]
+    acts = []
+    for i, (src, dst) in enumerate(zip(lefts, left_all)):
+        acts.append(
+            start(
+                remote(
+                    src,
+                    dst.at[pl.ds(half_tokens, half_tokens)],
+                    act_send.at[i],
+                    act_recv.at[i],
+                    "core",
+                )
+            )
+        )
+    for i, (src, dst) in enumerate(zip(rights, right_all)):
+        half = src.shape[1] // 2
+        theirs = pl.ds(pl.multiple_of((1 - core) * half, half), half)
+        acts.append(
+            start(
+                remote(
+                    src.at[:, theirs],
+                    dst.at[pl.ds(half_tokens, half_tokens)],
+                    act_send.at[n_left + i],
+                    act_recv.at[n_left + i],
+                    "core",
+                )
+            )
+        )
+    norm_dims = ("core",) + REDUCE_DIMS + ("xb",)
+    norm_copies = []
+
+    def norm_start(k):
+        if not with_norm:
+            return
+        if k < 6:
+            src, dst = (norm_held.at[k], norm_landed.at[k])
+        else:
+            src, dst = (norm_held.at[6, pl.ds(1 - shard, 1)], norm_landed.at[6, pl.ds(0, 1)])
+        norm_copies.append(
+            start(remote(src, dst, nrm_send.at[k], nrm_recv.at[k], norm_dims[k]))
+        )
+
+    def norm_finish(k):
+        if not with_norm:
+            return
+        norm_copies[k].wait_recv()
+        if k < 6:
+            norm_held[k + 1] = norm_held[k] + norm_landed[k]
+        else:
+            norm_out[...] = norm_held[6, shard] + norm_landed[6, 0]
+
+    if with_norm:
+        norm_held[0] = norm_in[...]
+    norm_start(0)
+    for src, dst in zip(lefts, left_all):
+        dst[pl.ds(0, half_tokens)] = src[...]
+    for src, dst in zip(rights, right_all):
+        half = src.shape[1] // 2
+        dst[pl.ds(0, half_tokens)] = src[:, pl.ds(pl.multiple_of(core * half, half), half)]
+    for copy in acts:
+        copy.wait_recv()
+    norm_finish(0)
+    norm_start(1)
+    edges = [0]
+    for width in widths:
+        edges.append(edges[-1] + width)
+    parts = range(len(widths))
+    cols = [pl.ds(edges[p], widths[p]) for p in parts]
+    orders = [rotated(REDUCE_DIMS, p) for p in parts]
+    starts = [row_starts(orders[p], ROWS) for p in parts]
+    moving = {}
+
+    def reduce_start(p, k):
+        if k < 5:
+            half = ROWS >> (k + 1)
+            away = pl.multiple_of(starts[p][k] + (half - (starts[p][k + 1] - starts[p][k])), 16)
+            src = partial.at[:, pl.ds(away, half), cols[p]]
+            dst = landed[k].at[:, :, cols[p]]
+            dim = orders[p][k]
+        else:
+            at = pl.multiple_of(starts[p][5], 16)
+            src = partial.at[1 - shard, pl.ds(at, 16), cols[p]]
+            dst = landed[5].at[:, cols[p]]
+            dim = "xb"
+        moving[p] = start(remote(src, dst, red_send.at[p, k], red_recv.at[p, k], dim))
+
+    def reduce_add(p, k):
+        moving[p].wait_recv()
+        if k < 5:
+            half = ROWS >> (k + 1)
+            step = min(half, 32)
+
+            def add(i, carry):
+                here = pl.ds(pl.multiple_of(i * step, step), step)
+                there = pl.ds(pl.multiple_of(starts[p][k + 1] + i * step, 16), step)
+                total = partial[:, there, cols[p]].astype(jnp.float32)
+                total = total + landed[k][:, here, cols[p]].astype(jnp.float32)
+                partial[:, there, cols[p]] = total.astype(jnp.bfloat16)
+                return carry
+
+            lax.fori_loop(0, half // step, add, 0)
+        else:
+            here = pl.ds(pl.multiple_of(starts[p][5], 16), 16)
+            total = partial[shard, here, cols[p]].astype(jnp.float32)
+            total = total + landed[5][:, cols[p]].astype(jnp.float32)
+            out[core, here, cols[p]] = total.astype(jnp.bfloat16)
+
+    ready = 0
+    for at, (left, left_step, left_off, right, right_off) in enumerate(dots):
+        for s in range(2):
+            product = lax.dot_general(
+                left_all[left][:, pl.ds(s * left_step + left_off, ROWS)],
+                right_all[right][:, pl.ds(right_off, 512)],
+                (((0,), (0,)), ((), ())),
+                preferred_element_type=jnp.float32,
+            )
+            partial[s, :, pl.ds(at * 512, 512)] = product.astype(jnp.bfloat16)
+        while ready < len(widths) and edges[ready + 1] <= (at + 1) * 512:
+            reduce_start(ready, 0)
+            ready += 1
+    for k in range(6):
+        norm_finish(k + 1)
+        if k < 5:
+            norm_start(k + 2)
+        for p in parts:
+            reduce_add(p, k)
+            if k < 5:
+                reduce_start(p, k + 1)
+
+    def range_of(p, at, size):
+        return out.at[core, pl.ds(pl.multiple_of(at, 16), size), cols[p]]
+
+    def gather_start(p, k):
+        mine = range_of(p, starts[p][k + 1], ROWS >> (k + 1))
+        moving[p] = start(
+            remote(mine, mine, gat_send.at[p, k], gat_recv.at[p, k], orders[p][k])
+        )
+
+    shared = []
+
+    def share(p, slot, at):
+        mine = range_of(p, at, ROWS // 2)
+        shared.append(
+            start(remote(mine, mine, gat_send.at[p, 5 + slot], gat_recv.at[p, 5 + slot], "core"))
+        )
+
+    for p in parts:
+        gather_start(p, 4)
+    for k in range(4, -1, -1):
+        for p in parts:
+            moving[p].wait_recv()
+            if k > 0:
+                gather_start(p, k - 1)
+            if k == 1:
+                share(p, 0, starts[p][1])
+            if k == 0:
+                share(p, 1, ROWS // 2 - starts[p][1])
+    for copy in shared:
+        copy.wait_recv()
+    for copy in sent:
+        copy.wait_send()
+
+
+def dots_rights(dots):
+    return sorted({d[3] for d in dots})
+
+
+def reduce_gradients(lefts, rights, dots, widths, norm, collective_id):
+    tokens = lefts[0].shape[0]
+    total = sum(widths)
+    out_shape = [jax.ShapeDtypeStruct((2, ROWS, total), jnp.bfloat16)]
+    scratch = [pltpu.VMEM((2 * tokens, a.shape[1]), jnp.bfloat16) for a in lefts]
+    scratch += [pltpu.VMEM((2 * tokens, a.shape[1] // 2), jnp.bfloat16) for a in rights]
+    scratch += [pltpu.VMEM((2, ROWS, total), jnp.bfloat16)]
+    scratch += [pltpu.VMEM((2, ROWS >> (k + 1), total), jnp.bfloat16) for k in range(5)]
+    scratch += [pltpu.VMEM((16, total), jnp.bfloat16)]
+    operands = [*lefts, *rights]
+    if norm is not None:
+        operands.append(norm)
+        out_shape.append(jax.ShapeDtypeStruct(norm.shape[1:], jnp.float32))
+        scratch += [
+            pltpu.VMEM((7, *norm.shape), jnp.float32),
+            pltpu.VMEM((7, *norm.shape), jnp.float32),
+        ]
+    n_act, parts = (len(lefts) + len(rights), len(widths))
+    scratch += [pltpu.SemaphoreType.DMA((n_act,))] * 2
+    scratch += [pltpu.SemaphoreType.DMA((parts, 6))] * 2
+    scratch += [pltpu.SemaphoreType.DMA((parts, 7))] * 2
+    scratch += [pltpu.SemaphoreType.DMA((7,))] * 2
+    return pl.pallas_call(
+        functools.partial(reduce_kernel, len(lefts), dots, widths, norm is not None),
+        out_shape=out_shape,
+        in_specs=[pl.BlockSpec(memory_space=pltpu.VMEM)] * len(operands),
+        out_specs=[pl.BlockSpec(memory_space=pltpu.VMEM)] * len(out_shape),
+        scratch_shapes=scratch,
+        compiler_params=pltpu.CompilerParams(
+            collective_id=collective_id, has_side_effects=True, vmem_limit_bytes=60 * 2**20
+        ),
+    )(*operands)
+
+
+FF_DOTS = tuple(
+    [(0, 512, 0, 0, j * 512) for j in range(4)]
+    + [(1, 2048, q * 512, 1, 0) for q in range(4)]
+    + [(2, 512, 0, 2, 0)]
+)
+FF_WIDTHS = (1024, 896, 896, 896, 896)
+QKV_DOTS = ((0, 512, 0, 0, 0), (0, 512, 0, 1, 0), (0, 512, 0, 2, 0))
+QKV_WIDTHS = (384, 384, 256, 256, 256)
+
+
+def cast_kernel(x_ref, o_ref):
+    o_ref[...] = x_ref[0].astype(jnp.float32)
+
+
+def cast_out(gathered, shape, grid, index_in, index_out):
+    return pl.pallas_call(
+        cast_kernel,
+        out_shape=jax.ShapeDtypeStruct(shape, jnp.float32),
+        grid=grid,
+        in_specs=[pl.BlockSpec((1, ROWS, 512), index_in)],
+        out_specs=pl.BlockSpec((ROWS, 512), index_out),
+    )(gathered)
+
+
+def square_out(gathered, slot):
+    return cast_out(gathered, (ROWS, 1024), (2,), lambda c: (c, 0, slot), lambda c: (0, c))
+
+
+def ff_grads_out(gathered):
+    grad_in = cast_out(
+        gathered, (ROWS, 4096), (2, 4), lambda c, j: (c, 0, j), lambda c, j: (0, c * 4 + j)
+    )
+    grad_down = cast_out(
+        gathered, (2048, 1024), (4, 2), lambda q, c: (c, 0, 4 + q), lambda q, c: (q, c)
+    )
+    return (grad_in, grad_down, square_out(gathered, 8))
 
 
 def normalize(summed_in, norm_gain, norm_bias):
@@ -114,26 +520,18 @@
     norm2_bias,
     cotangent,
 ):
-    gathered = (
-        *sent_together(
-            (w_query, w_key, w_value, w_out, norm1_gain, norm1_bias, w_in), "shard", 0, 1
-        ),
-        lax.all_gather(w_down, "shard", axis=0, tiled=True),
-        lax.all_gather(norm2_gain, "shard", axis=0, tiled=True),
-        lax.all_gather(norm2_bias, "shard", axis=0, tiled=True),
-    )
-    (
-        full_query,
-        full_key,
-        full_value,
-        full_out,
-        gain_one,
-        bias_one,
-        full_in,
-        full_down,
-        gain_two,
-        bias_two,
-    ) = gathered
+    packed = jnp.zeros((16, 512), jnp.bfloat16).at[:4].set(
+        jnp.stack([norm1_gain, norm1_bias, norm2_gain, norm2_bias])
+    )
+    full_qkv, full_out, full_in, full_down = gather_weights(
+        [w_query, w_key, w_value, w_out, w_in, w_down],
+        [(0, 0), (0, 1024), (0, 2048), (1, 0), (2, 0), (3, 0)],
+        [(1024, 3072), (1024, 1024), (1024, 4096), (4096, 1024)],
+        0,
+    )
+    full_query, full_key, full_value = jnp.split(full_qkv, 3, axis=1)
+    norms = lax.all_gather(packed, "shard", axis=1, tiled=True)[:4]
+    gain_one, bias_one, gain_two, bias_two = norms
     gain_one = gain_one.astype(jnp.float32)
     bias_one = bias_one.astype(jnp.float32)
     gain_two = gain_two.astype(jnp.float32)
@@ -228,11 +626,9 @@
     upstream = cotangent[0].astype(jnp.float32)
     grad_two, grad_gain_two, grad_bias_two = normalize_back(upstream, scaled_two, inv_two, gain_two)
     ff_grad = grad_two.astype(jnp.bfloat16)
-    grad_down = jnp.einsum("tf,td->fd", hidden, ff_grad, preferred_element_type=jnp.float32)
     hidden_grad = jnp.einsum("td,fd->tf", ff_grad, full_down, preferred_element_type=jnp.float32)
     gelu_pull = jax.vjp(exact_gelu, pre)[1]
     pre_grad = gelu_pull(hidden_grad)[0].astype(jnp.bfloat16)
-    grad_in = jnp.einsum("td,tf->df", first_low, pre_grad, preferred_element_type=jnp.float32)
     first_grad = grad_two + jnp.einsum(
         "tf,df->td", pre_grad, full_in, preferred_element_type=jnp.float32
     )
@@ -240,7 +636,17 @@
         first_grad, scaled_one, inv_one, gain_one
     )
     attn_grad = grad_one.astype(jnp.bfloat16)
-    grad_out_weight = jnp.einsum("tc,td->cd", mixed, attn_grad, preferred_element_type=jnp.float32)
+    norm_sums = jnp.stack([grad_gain_one, grad_bias_one, grad_gain_two, grad_bias_two])
+    norm_sums = jnp.pad(norm_sums.reshape(4, 2, 512).transpose(1, 0, 2), ((0, 0), (0, 4), (0, 0)))
+    ff_summed, norm_total = reduce_gradients(
+        [first_low, hidden, mixed],
+        [pre_grad, ff_grad, attn_grad],
+        FF_DOTS,
+        FF_WIDTHS,
+        norm_sums,
+        1,
+    )
+    grad_in, grad_down, grad_out_weight = ff_grads_out(ff_summed)
     mixed_grad = jnp.einsum(
         "td,cd->tc", attn_grad, full_out, preferred_element_type=jnp.float32
     ).astype(jnp.bfloat16)
@@ -329,107 +735,22 @@
     input_grad = input_grad + jnp.einsum(
         "td,cd->tc", value_tok, full_value, preferred_element_type=jnp.float32
     )
-    weight_grads = (
-        jnp.einsum("tc,td->cd", token_rows, query_tok, preferred_element_type=jnp.float32),
-        jnp.einsum("tc,td->cd", token_rows, key_tok, preferred_element_type=jnp.float32),
-        jnp.einsum("tc,td->cd", token_rows, value_tok, preferred_element_type=jnp.float32),
-        grad_out_weight,
-        grad_gain_one,
-        grad_bias_one,
-        grad_in,
-        grad_down,
-        grad_gain_two,
-        grad_bias_two,
-    )
-    halves = (
-        *tuple(
-            (
-                part.astype(jnp.float32)
-                for part in side_by_side(
-                    (
-                        weight_grads[0].astype(jnp.bfloat16),
-                        weight_grads[1].astype(jnp.bfloat16),
-                        weight_grads[2].astype(jnp.bfloat16),
-                        weight_grads[3].astype(jnp.bfloat16),
-                        weight_grads[4].astype(jnp.bfloat16),
-                        weight_grads[5].astype(jnp.bfloat16),
-                        weight_grads[6].astype(jnp.bfloat16),
-                    ),
-                    "shard",
-                    0,
-                    1,
-                )
-            )
-        ),
-        lax.psum_scatter(
-            weight_grads[7].astype(jnp.bfloat16), "shard", scatter_dimension=0, tiled=True
-        ).astype(jnp.float32),
-        lax.psum_scatter(
-            weight_grads[8].astype(jnp.bfloat16), "shard", scatter_dimension=0, tiled=True
-        ).astype(jnp.float32),
-        lax.psum_scatter(
-            weight_grads[9].astype(jnp.bfloat16), "shard", scatter_dimension=0, tiled=True
-        ).astype(jnp.float32),
-    )
-    pieces = one_scatter(
-        (
-            halves[0],
-            halves[1],
-            halves[2],
-            halves[3],
-            halves[4],
-            halves[5],
-            halves[6],
-            halves[7],
-            halves[8],
-            halves[9],
-        ),
-        ("blk", "aa"),
-        (0, 0, 0, 0, 0, 0, 0, 0, 0, 0),
-    )
-    shares = (
-        *tuple(
-            (
-                part.astype(jnp.float32)
-                for part in sent_together(
-                    (
-                        pieces[0].astype(jnp.bfloat16),
-                        pieces[1].astype(jnp.bfloat16),
-                        pieces[2].astype(jnp.bfloat16),
-                        pieces[3].astype(jnp.bfloat16),
-                        pieces[4].astype(jnp.bfloat16),
-                        pieces[5].astype(jnp.bfloat16),
-                        pieces[6].astype(jnp.bfloat16),
-                    ),
-                    ("blk", "aa"),
-                    0,
-                    1,
-                )
-            )
-        ),
-        lax.all_gather(pieces[7].astype(jnp.bfloat16), ("blk", "aa"), axis=0, tiled=True).astype(
-            jnp.float32
-        ),
-        lax.all_gather(pieces[8].astype(jnp.bfloat16), ("blk", "aa"), axis=0, tiled=True).astype(
-            jnp.float32
-        ),
-        lax.all_gather(pieces[9].astype(jnp.bfloat16), ("blk", "aa"), axis=0, tiled=True).astype(
-            jnp.float32
-        ),
-    )
+    qkv_summed = reduce_gradients(
+        [token_rows], [query_tok, key_tok, value_tok], QKV_DOTS, QKV_WIDTHS, None, 2
+    )[0]
     return (
         result.astype(jnp.bfloat16)[None],
         input_grad.astype(jnp.bfloat16)[None],
-        shares[0],
-        shares[1],
-        shares[2],
-        shares[3],
-        shares[4],
-        shares[5],
-        shares[6],
-        shares[7],
-        shares[8],
-        shares[9],
+        square_out(qkv_summed, 0),
+        square_out(qkv_summed, 1),
+        square_out(qkv_summed, 2),
+        grad_out_weight,
+        norm_total[0],
+        norm_total[1],
+        grad_in,
+        grad_down,
+        norm_total[2],
+        norm_total[3],
     )
 
 

time: 1750 us -> 959 us (0.55)
  waiting for transfers between devices: 971 us -> 44.4 us
  Pallas kernels: 0 us -> 584 us
  local copies, waits for them, and re-layouts: 255 us -> 53.9 us
  blocking collectives: 145 us -> 5.47 us
  other arithmetic: 75.3 us -> 36.2 us
  matrix products: 206 us -> 168 us
    pallas_call x0 -> x9, Pallas kernels: none -> 584 us  [the longest x1 390 us: gather_weights(): pl.pallas_call(functools.partial(gather_kernel, shapes, targets, len(out_...]
    all_gather x4 -> x0, waiting for transfers between devices: 394 us -> none  [the longest x2 375 us: sent_together(): filled = lax.all_gather(both, axis, axis=dim, tiled=True)]
    unnamed x8 -> x0, waiting for transfers between devices: 336 us -> none
    reduce_scatter x2 -> x0, waiting for transfers between devices: 182 us -> none  [the longest x1 182 us: side_by_side(): lax.psum_scatter(both, axis, scatter_dimension=dim, tiled=True)]
    unnamed x2 -> x0, blocking collectives: 135 us -> none
    unnamed x171 -> x110, local copies, waits for them, and re-layouts: 80.6 us -> 8.13 us
    concatenate x4 -> x0, local copies, waits for them, and re-layouts: 49.9 us -> none  [the longest x1 31 us: side_by_side(): both = jnp.concatenate(columns, axis=along)]
    dot_general x6 -> x0, matrix products: 21.1 us -> none  [the longest x1 7.09 us: shards(): jnp.einsum('td,tf->df', first_low, pre_grad, preferred_element_type=jnp.f...]
  transfers between devices with their start and end apart: 18 -> 11, of which waited for: 11 -> 7; matrix products, arithmetic and copies ran while one was open for 16% -> 6% of each run, Pallas kernels for 0% -> 13%
where the time goes in v1:
time: 959 us; the launch traced here: 949 us
  Pallas kernels  584 us (61%)
  matrix products  168 us (18%)
  local copies, waits for them, and re-layouts  53.9 us (6%)
  waiting for transfers between devices  44.4 us (5%)
  other arithmetic  36.2 us (4%)
  starting transfers between devices  32.5 us (3%)
  loops' own time  23 us (2%)
    pallas_call x1, Pallas kernels, gather_weights(): pl.pallas_call(functools.partial(gather_kernel, shapes, targets, len(out_...  390 us
    pallas_call x2, Pallas kernels, reduce_gradients(): pl.pallas_call(functools.partial(reduce_kernel, len(lefts), dots, widths,...  169 us
    dot_general x16, matrix products, visit(): jnp.einsum('qhd,khd->hqk', query_block, key_heads, preferred_element_type...  33.7 us
    dot_general x16, matrix products, attend_visit(): jnp.einsum('qhd,khd->hqk', query_block, attend_key_heads, preferred_eleme...  30.6 us
    pallas_call x6, Pallas kernels, cast_out(): pl.pallas_call(cast_kernel, out_shape=jax.ShapeDtypeStruct(shape, jnp.flo...  24.4 us
    ppermute x7, waiting for transfers between devices, from_behind(): lax.ppermute(value, axis, [(i, (i + by) % devices) for i in range(devices)])  23 us
    dot_general x16, matrix products, visit(): jnp.einsum('hqk,khd->qhd', score_grad, key_heads, preferred_element_type=...  21.5 us
    dynamic_slice x48, local copies, waits for them, and re-layouts, shards(): state = lax.map(attend_visit, (block_ids, q_blocks) + state)  19.2 us
  transfers between devices with their start and end apart: 11, of which 7 were waited for; matrix products, arithmetic and copies ran while one was open for 6% of the time, Pallas kernels for 13%

profile of v1, /device:TPU:1, one launch (start us, length us, event | category | flops | bytes accessed | tf_op | source)
XLA Modules:
  0.0 949.5 jit_solution(14010821096716443391)
XLA Ops:
  0.7 390.1 %shard_map.229 = (bf16[1024,3072]{1,0:T(8,128)(2,1)}, bf16[1024,1024]{1,0:T(8,128)(2,1)}, bf16[1024,4096]{1,0:T(8,128)(2,1)}, bf16[4096,1024]{1,0:T(8,128)(2,1)}) custom-call(bf16[512,1024]{1,0:T(8,128)(2,1)} %refs_0_.1, bf16[512,1024]{1,0:T(8,128)(2,1)} %refs_1_.1, bf16[512,1024]{1,0:T(8,128)(2,1)} %refs_2_.1, bf16[512,1024]{1,0:T(8,128)(2,1)} %refs_3_.1, ...), custom_call_target="tpu_custom_call" | custom-call | tf_op jit(solution)/shard_map/pallas_call | solution.py:190
  398.8 6.4 all-to-all-start
  407.7 10.4 %all-to-all-done = bf16[128,16,192]{0,2,1:T(8,128)(2,1)S(1)} async-done(((bf16[128,16,192]{0,2,1:T(8,128)(2,1)}), bf16[128,16,192]{0,2,1:T(8,128)(2,1)S(1)}, u32[]{:S(2)}, u32[]{:S(2)}) %all-to-all-start) | async-done | bytes 786464 | tf_op jit(solution)/shard_map/all_to_all | solution.py:559
  423.3 22.4 %while.122 = (s32[]{:T(128)}, f32[4,1,512]{2,1,0:T(1,128)S(1)}, f32[4,1,512]{2,1,0:T(1,128)S(1)}, f32[4,512,1,64]{1,3,2,0:T(8,128)S(1)}, s32[4]{0:T(128)S(1)}, /...) while((s32[]{:T(128)}, f32[4,1,512]{2,1,0:T(1,128)S(1)}, ...), condition=%wide.region_3.4_spmd, body=%wide.region_0.3_spmd.sunk | while | flops 280009216 | bytes 13375747 | solution.py:606
  446.3 18.7 %while.123 = (s32[]{:T(128)}, f32[4,1,512]{2,1,0:T(1,128)S(1)}, f32[4,1,512]{2,1,0:T(1,128)S(1)}, f32[4,512,1,64]{1,3,2,0:T(8,128)S(1)}, f32[4,1,512]{2,1,0:T(1,...) while((s32[]{:T(128)}, f32[4,1,512]{2,1,0:T(1,128)S(1)}, ...), condition=%wide.region_7.8_spmd, body=%wide.region_4.7_spmd.sunk | while | flops 280042496 | bytes 13519135 | solution.py:606
  468.7 18.7 %while.124 = (s32[]{:T(128)}, f32[4,1,512]{2,1,0:T(1,128)S(1)}, f32[4,1,512]{2,1,0:T(1,128)S(1)}, f32[4,512,1,64]{1,3,2,0:T(8,128)S(1)}, f32[4,1,512]{2,1,0:T(1,...) while((s32[]{:T(128)}, f32[4,1,512]{2,1,0:T(1,128)S(1)}, ...), condition=%wide.region_11.12_spmd, body=%wide.region_8.11_spmd.sunk | while | flops 280042496 | bytes 13519135 | solution.py:606
  488.8 24.4 %while.125 = (s32[]{:T(128)}, f32[4,1,512]{2,1,0:T(1,128)S(1)}, f32[4,1,512]{2,1,0:T(1,128)S(1)}, f32[4,512,1,64]{1,0,3,2:T(4,128)S(1)}, f32[4,1,512]{2,1,0:T(1,...) while((s32[]{:T(128)}, f32[4,1,512]{2,1,0:T(1,128)S(1)}, ...), condition=%wide.region_15.16_spmd, body=%wide.region_12.15_spmd.sunk | while | flops 280042496 | bytes 14043427 | solution.py:606
  519.8 5.5 all_gather.3
  532.1 9.2 multiply_convert_fusion.4
  544.9 5.1 add_convert_fusion.refs_3_
  557.1 3.9 all-to-all-start.2
  561.0 8.2 all-to-all-done.2
  570.7 45.3 %while.129 = (s32[]{:T(128)}, f32[2048,2,1,64]{0,3,2,1:T(8,128)}, f32[4,512,1,64]{1,3,2,0:T(8,128)}, bf16[4,512,1,64]{1,3,2,0:T(8,128)(2,1)S(1)}, s32[4]{0:T(128...) while((s32[]{:T(128)}, f32[2048,2,1,64]{0,3,2,1:T(8,128)}, ...), condition=%wide.region_26.27_spmd.clone, body=%wide.region_25.26_spmd.clone.sunk | while | flops 683577856 | bytes 28502424 | solution.py:709
  619.7 6.1 collective-permute-done.3
  626.0 24.1 %while.126 = (s32[]{:T(128)}, f32[2048,2,1,64]{0,3,2,1:T(8,128)S(1)}, f32[4,512,1,64]{1,3,2,0:T(8,128)S(1)}, bf16[4,512,1,64]{1,3,2,0:T(8,128)(2,1)S(1)}, s32[4]...) while((s32[]{:T(128)}, ...), condition=%wide.region_28.29_spmd, body=%wide.region_27.28_spmd.sunk | while | flops 683315712 | bytes 24308000 | solution.py:709
  653.0 6.1 collective-permute-done.4
  660.4 24.1 %while.127 = (s32[]{:T(128)}, f32[2048,2,1,64]{0,3,2,1:T(8,128)S(1)}, f32[4,512,1,64]{1,3,2,0:T(8,128)S(1)}, bf16[4,512,1,64]{1,3,2,0:T(8,128)(2,1)S(1)}, s32[4]...) while((s32[]{:T(128)}, ...), condition=%wide.region_30.31_spmd, body=%wide.region_29.30_spmd.sunk | while | flops 683315712 | bytes 24308000 | solution.py:709
  688.0 6.4 collective-permute-done.5
  696.5 26.7 %while.128 = (s32[]{:T(128)}, f32[2048,2,1,64]{0,3,2,1:T(8,128)S(1)}, f32[4,512,1,64]{1,3,2,0:T(8,128)}, bf16[4,512,1,64]{1,3,2,0:T(8,128)(2,1)S(1)}, s32[4]{0:T...) while((s32[]{:T(128)}, ...), condition=%wide.region_32.33_spmd, body=%wide.region_31.32_spmd.sunk | while | flops 683315712 | bytes 24308000 | solution.py:709
  727.6 4.3 collective-permute-done.6
  741.2 106.6 %shard_map.234 = (bf16[2,512,4608]{2,1,0:T(8,128)(2,1)}, f32[8,512]{1,0:T(8,128)}) custom-call(bf16[128,1024]{1,0:T(8,128)(2,1)} %copy-done.28, bf16[128,4096]{1,0:T(8,128)(2,1)} %copy-done.17, bf16[128,1024]{1,0:T(8,128)(2,1)} %copy.146.refs_2_, bf16[128,4096]{1,0:T(8,128)(2,1)} %copy-done.18, bf16[128,1024]{1,0:T(8,128)(2,1)} %copy-done.27, ...), custom_call_target="tpu_custom_call" | custom-call | tf_op jit(solution)/shard_map/pallas_call | solution.py:420
  850.3 7.3 shard_map.236
  857.6 7.3 shard_map.237
  876.0 62.5 %shard_map.230.x_ref = bf16[2,512,1536]{2,1,0:T(8,128)(2,1)} custom-call(bf16[128,1024]{1,0:T(8,128)(2,1)} %bitcast.686, bf16[128,1024]{1,0:T(8,128)(2,1)} %copy.143.refs_1_, bf16[128,1024]{1,0:T(8,128)(2,1)} %copy.144.refs_2_, bf16[128,1024]{1,0:T(8,128)(2,1)} %copy.145.refs_3_), custom_call_target="tpu_custom_call" | custom-call | tf_op jit(solution)/shard_map/pallas_call | solution.py:420
  (635 shorter events, 278.5 us)
Async XLA Ops:
  0.6 390.1 %copy-start.29 = (bf16[1,128,1024]{2,1,0:T(8,128)(2,1)S(1)}, bf16[1,128,1024]{2,1,0:T(8,128)(2,1)}, u32[]{:S(2)}) copy-start(bf16[1,128,1024]{2,1,0:T(8,128)(2,1)} %param.32) | copy-start | bytes 786436
  398.8 19.3 %all-to-all-start = ((bf16[128,16,192]{0,2,1:T(8,128)(2,1)}), bf16[128,16,192]{0,2,1:T(8,128)(2,1)S(1)}, u32[]{:S(2)}, u32[]{:S(2)}) async-start(bf16[128,16,192]{0,2,1:T(8,128)(2,1)} %pad_maximum_fusion), calls=%async_computation | async-start | bytes 1572864 | tf_op jit(solution)/shard_map/all_to_all | solution.py:559
  420.8 24.8 %collective-permute-start = (bf16[2048,2,1,64]{0,3,1,2:T(8,128)(2,1)}, bf16[2048,2,1,64]{0,3,1,2:T(8,128)(2,1)S(1)}, u32[]{:S(2)}, u32[]{:S(2)}) collective-permute-start(bf16[2048,2,1,64]{0,3,1,2:T(8,128)(2,1)} %slice.102), channel_id=1, source_target_pairs={{0,16},{16,32},{32,48},{48,0},{1,17},{17,33},{33,49},{49,1},{2,18}... | collective-permute-start | bytes 1572872 | tf_op jit(solution)/shard_map/ppermute | solution.py:22
  445.7 20.0 %collective-permute-start.1 = (bf16[2048,2,1,64]{0,3,1,2:T(8,128)(2,1)S(1)}, bf16[2048,2,1,64]{0,3,1,2:T(8,128)(2,1)}, u32[]{:S(2)}, u32[]{:S(2)}) collective-permute-start(bf16[2048,2,1,64]{0,3,1,2:T(8,128)(2,1)S(1)} %collective-permute-done), channel_id=1, source_target_pairs={{0,16},{16,32},{32,48},{48,0},{1,17},{17,33},{33,49},{49,1},{2,18}... | collective-permute-start | bytes 1572872 | tf_op jit(solution)/shard_map/ppermute | solution.py:22
  466.9 20.6 %collective-permute-start.2 = (bf16[2048,2,1,64]{0,3,1,2:T(8,128)(2,1)}, bf16[2048,2,1,64]{0,3,1,2:T(8,128)(2,1)}, u32[]{:S(2)}, u32[]{:S(2)}) collective-permute-start(bf16[2048,2,1,64]{0,3,1,2:T(8,128)(2,1)} %collective-permute-done.1), channel_id=1, source_target_pairs={{0,16},{16,32},{32,48},{48,0},{1,17},{17,33},{33,49},{49,1},{2,18}... | collective-permute-start | bytes 1572872 | tf_op jit(solution)/shard_map/ppermute | solution.py:22
  513.2 15.4 %copy-start.6 = (bf16[2048,1,64]{0,2,1:T(8,128)(2,1)}, bf16[2048,1,64]{0,2,1:T(8,128)(2,1)S(1)}, u32[]{:S(2)}) copy-start(bf16[2048,1,64]{0,2,1:T(8,128)(2,1)S(1)} %get-tuple-element.3652) | copy-start | bytes 786436
  513.2 15.4 %copy-start.14 = (bf16[2048,1,64]{0,2,1:T(8,128)(2,1)}, bf16[2048,1,64]{0,2,1:T(8,128)(2,1)S(1)}, u32[]{:S(2)}) copy-start(bf16[2048,1,64]{0,2,1:T(8,128)(2,1)S(1)} %get-tuple-element.3662) | copy-start | bytes 786436
  513.2 15.4 %copy-start.30 = (s32[2048]{0:T(1024)}, s32[2048]{0:T(1024)S(1)}, u32[]{:S(2)}) copy-start(s32[2048]{0:T(1024)S(1)} %get-tuple-element.3667) | copy-start | bytes 24580
  513.2 15.4 %copy-start.37 = (s32[2048]{0:T(1024)}, s32[2048]{0:T(1024)S(1)}, u32[]{:S(2)}) copy-start(s32[2048]{0:T(1024)S(1)} %get-tuple-element.3691) | copy-start | bytes 24580
  516.2 11.7 %all-to-all-start.1 = ((bf16[16,2,4096]{2,1,0:T(2,128)(2,1)}), bf16[16,2,4096]{2,1,0:T(2,128)(2,1)S(1)}, u32[]{:S(2)}, u32[]{:S(2)}) async-start(bf16[16,2,4096]{2,1,0:T(2,128)(2,1)} %reshape.1064), calls=%async_computation.1 | async-start | bytes 524288 | tf_op jit(solution)/shard_map/all_to_all | solution.py:610
  529.2 20.7 %slice-start.2 = ((s8[8388608]{0:T(1024)(128)(4,1)}), s8[4194304]{0:T(1024)(128)(4,1)S(1)}, s32[]{:S(2)}) async-start(s8[8388608]{0:T(1024)(128)(4,1)} %bitcast.667), calls=%async_computation.6 | async-start | bytes 8388608
  529.3 12.0 %slice-start = ((s8[8388608]{0:T(1024)(128)(4,1)}), s8[4194304]{0:T(1024)(128)(4,1)S(1)}, s32[]{:S(2)}) async-start(s8[8388608]{0:T(1024)(128)(4,1)} %bitcast.665), calls=%async_computation.4 | async-start | bytes 8388608
  532.1 17.9 %slice-start.3 = ((s8[8388608]{0:T(1024)(128)(4,1)}), s8[4194304]{0:T(1024)(128)(4,1)S(1)}, s32[]{:S(2)}) async-start(s8[8388608]{0:T(1024)(128)(4,1)} %bitcast.667), calls=%async_computation.7 | async-start | bytes 8388608
  556.2 14.4 %copy-start.40 = (s32[2048]{0:T(1024)S(1)}, s32[2048]{0:T(1024)}, u32[]{:S(2)}) copy-start(s32[2048]{0:T(1024)} %copy-done.39) | copy-start | bytes 24580
  557.1 12.1 %all-to-all-start.2 = ((bf16[128,16,64]{0,2,1:T(8,128)(2,1)}), bf16[128,16,64]{0,2,1:T(8,128)(2,1)S(1)}, u32[]{:S(2)}, u32[]{:S(2)}) async-start(bf16[128,16,64]{0,2,1:T(8,128)(2,1)} %bitcast.131), calls=%async_computation.2 | async-start | bytes 524288 | tf_op jit(solution)/shard_map/all_to_all | solution.py:653
  617.3 8.5 collective-permute-start.3
  650.2 8.9 collective-permute-start.4
  684.5 11.9 %copy-start.25 = (f32[4,512,1,64]{1,3,2,0:T(8,128)}, f32[4,512,1,64]{1,3,2,0:T(8,128)S(1)}, u32[]{:S(2)}) copy-start(f32[4,512,1,64]{1,3,2,0:T(8,128)S(1)} %get-tuple-element.1433) | copy-start | bytes 1572868
  684.5 11.9 %copy-start.7 = (bf16[2048,1,64]{0,2,1:T(8,128)(2,1)S(1)}, bf16[2048,1,64]{0,2,1:T(8,128)(2,1)}, u32[]{:S(2)}) copy-start(bf16[2048,1,64]{0,2,1:T(8,128)(2,1)} %copy-done.6) | copy-start | bytes 786436
  684.5 11.9 %copy-start.15 = (bf16[2048,1,64]{0,2,1:T(8,128)(2,1)S(1)}, bf16[2048,1,64]{0,2,1:T(8,128)(2,1)}, u32[]{:S(2)}) copy-start(bf16[2048,1,64]{0,2,1:T(8,128)(2,1)} %copy-done.14) | copy-start | bytes 786436
  685.4 9.0 collective-permute-start.5
  696.5 29.3 %copy-start.24 = (f32[4,512,1,64]{1,3,2,0:T(8,128)S(1)}, f32[4,512,1,64]{1,3,2,0:T(8,128)}, u32[]{:S(2)}) copy-start(f32[4,512,1,64]{1,3,2,0:T(8,128)} %get-tuple-element.1429) | copy-start | bytes 1572868
  723.2 8.7 collective-permute-start.6
  735.8 129.7 %all-to-all-start.3 = ((bf16[16,2,12288]{2,1,0:T(2,128)(2,1)}), bf16[16,2,12288]{2,1,0:T(2,128)(2,1)S(1)}, u32[]{:S(2)}, u32[]{:S(2)}) async-start(bf16[16,2,12288]{2,1,0:T(2,128)(2,1)} %reshape.1066), calls=%async_computation.3 | async-start | bytes 1572864 | tf_op jit(solution)/shard_map/all_to_all | solution.py:717
  (53 other events, 289.9 us)

commit v2 on v1

--- a/solution.py
+++ b/solution.py
@@ -1,5 +1,4 @@
 import functools
-import math
 
 import jax
 import jax.numpy as jnp
@@ -10,16 +9,204 @@
 
 HEADS = 16
 HEAD = 64
-QBLK = 512
-
-
 MASKED_SCORE = -1e30
 NORM_EPSILON = 1e-05
-
-
-def from_behind(value, axis, by):
-    devices = lax.axis_size(axis)
-    return lax.ppermute(value, axis, [(i, (i + by) % devices) for i in range(devices)])
+QUERY_BLOCK = 512
+PARTS = 1
+BLOCK_LEN = 2048
+KEY_BLOCK = 1024
+
+
+def spans(segments, valid):
+    numbers = jnp.arange(36, dtype=jnp.int32)
+    before = jnp.sum((segments[None, :] < numbers[:, None]).astype(jnp.int32), axis=1)
+    live = jnp.sum(valid)
+    picked = segments[:, None] == numbers[None, :35]
+    first = jnp.sum(jnp.where(picked, before[None, :35], 0), axis=1)
+    last = jnp.sum(jnp.where(picked, before[None, 1:], 0), axis=1)
+    return (first, last, jnp.minimum(last, live))
+
+
+def block_plan(first, last, live, query_start, count):
+    mine = [lax.dynamic_slice_in_dim(a, query_start, count) for a in (first, last, live)]
+    low = mine[0].reshape(-1, QUERY_BLOCK)
+    high = mine[1].reshape(-1, QUERY_BLOCK)
+    end = mine[2].reshape(-1, QUERY_BLOCK)
+    begin = low[:, 0] // KEY_BLOCK
+    stop = -(-high[:, -1] // KEY_BLOCK)
+    single = low[:, 0] == low[:, -1]
+    full_from = -(-low[:, 0] // KEY_BLOCK)
+    full_to = end[:, 0] // KEY_BLOCK
+    some = single & (full_to > full_from)
+    full_from = jnp.where(some, full_from, stop)
+    full_to = jnp.where(some, full_to, stop)
+    return (jnp.stack([begin, full_from, full_to, stop]), mine[0], mine[2])
+
+
+def slot_of(j, blk):
+    per = BLOCK_LEN // KEY_BLOCK
+    at = ((j // per) ^ blk) * per + j % per
+    return pl.ds(pl.multiple_of(at * KEY_BLOCK, KEY_BLOCK), KEY_BLOCK)
+
+
+def attend_kernel(plan_ref, start_ref, q_ref, kv_ref, kvt_ref, low_ref, end_ref, o_ref, lse_ref):
+    i = pl.program_id(0)
+    low, end = (low_ref[0:1], end_ref[0:1])
+    place_q = start_ref[0] + i * QUERY_BLOCK + lax.broadcasted_iota(jnp.int32, (1, QUERY_BLOCK), 1)
+    split = QUERY_BLOCK // PARTS
+
+    def step(j, carry, masked):
+        here = slot_of(j, start_ref[1])
+        keys = kv_ref[here]
+        keys_t = kvt_ref[:, here]
+        done = []
+        for part, (top, total, summed) in enumerate(carry):
+            cols = slice(part * split, (part + 1) * split)
+            scores = lax.dot_general(
+                keys, q_ref[cols], (((1,), (1,)), ((), ())), preferred_element_type=jnp.float32
+            )
+            if masked:
+                place_k = j * KEY_BLOCK + lax.broadcasted_iota(jnp.int32, scores.shape, 0)
+                allowed = (place_k >= low[:, cols]) & (place_k < end[:, cols])
+                allowed = allowed | (place_k == place_q[:, cols])
+                scores = jnp.where(allowed, scores, MASKED_SCORE)
+            new_top = jnp.maximum(top, jnp.max(scores, axis=0, keepdims=True))
+            weights = jnp.exp(scores - new_top)
+            factor = jnp.exp(top - new_top)
+            total = total * factor + jnp.sum(weights, axis=0, keepdims=True)
+            summed = summed * factor + jnp.dot(
+                keys_t, weights.astype(jnp.bfloat16), preferred_element_type=jnp.float32
+            )
+            done.append((new_top, total, summed))
+        return tuple(done)
+
+    carry = tuple(
+        (
+            jnp.full((1, split), MASKED_SCORE, jnp.float32),
+            jnp.zeros((1, split), jnp.float32),
+            jnp.zeros((128, split), jnp.float32),
+        )
+        for _ in range(PARTS)
+    )
+    masked_step = functools.partial(step, masked=True)
+    carry = lax.fori_loop(plan_ref[0, i], plan_ref[1, i], masked_step, carry)
+    carry = lax.fori_loop(
+        plan_ref[1, i], plan_ref[2, i], functools.partial(step, masked=False), carry
+    )
+    carry = lax.fori_loop(plan_ref[2, i], plan_ref[3, i], masked_step, carry)
+    for part, (top, total, summed) in enumerate(carry):
+        cols = slice(part * split, (part + 1) * split)
+        o_ref[cols] = jnp.transpose(summed / total)
+        lse_ref[:, cols] = jnp.broadcast_to(top + jnp.log(total), (8, split))
+
+
+def attend(plan, query_start, queries, pairs, low, end):
+    count = queries.shape[0]
+    blocks = count // QUERY_BLOCK
+    row = pl.BlockSpec((8, QUERY_BLOCK), lambda i, *_: (0, i))
+    return pl.pallas_call(
+        attend_kernel,
+        out_shape=[
+            jax.ShapeDtypeStruct((count, 128), jnp.float32),
+            jax.ShapeDtypeStruct((8, count), jnp.float32),
+        ],
+        grid_spec=pltpu.PrefetchScalarGridSpec(
+            num_scalar_prefetch=2,
+            grid=(blocks,),
+            in_specs=[
+                pl.BlockSpec((QUERY_BLOCK, 128), lambda i, *_: (i, 0)),
+                pl.BlockSpec(pairs.shape, lambda i, *_: (0, 0)),
+                pl.BlockSpec(pairs.shape[::-1], lambda i, *_: (0, 0)),
+                row,
+                row,
+            ],
+            out_specs=[pl.BlockSpec((QUERY_BLOCK, 128), lambda i, *_: (i, 0)), row],
+        ),
+        compiler_params=pltpu.CompilerParams(vmem_limit_bytes=56 * 2**20),
+    )(
+        plan,
+        query_start,
+        queries,
+        pairs,
+        pairs.T,
+        jnp.broadcast_to(low[None], (8, count)),
+        jnp.broadcast_to(end[None], (8, count)),
+    )
+
+
+def attend_back_kernel(
+    plan_ref, start_ref, q_ref, g_ref, kv_ref, kvt_ref, low_ref, end_ref, lse_ref, delta_ref, dq_ref, dkv_ref
+):
+    i = pl.program_id(0)
+
+    @pl.when(i == 0)
+    def _():
+        dkv_ref[...] = jnp.zeros_like(dkv_ref)
+
+    queries, upstream = (q_ref[...], g_ref[...])
+    low, end = (low_ref[0:1], end_ref[0:1])
+    lse, delta = (lse_ref[0:1], delta_ref[0:1])
+    place_q = start_ref[0] + i * QUERY_BLOCK + lax.broadcasted_iota(jnp.int32, (1, QUERY_BLOCK), 1)
+
+    def step(j, query_grad, masked):
+        here = slot_of(j, start_ref[1])
+        keys = kv_ref[here]
+        scores = lax.dot_general(
+            keys, queries, (((1,), (1,)), ((), ())), preferred_element_type=jnp.float32
+        )
+        if masked:
+            place_k = j * KEY_BLOCK + lax.broadcasted_iota(jnp.int32, scores.shape, 0)
+            allowed = ((place_k >= low) & (place_k < end)) | (place_k == place_q)
+            scores = jnp.where(allowed, scores, MASKED_SCORE)
+        probs = jnp.exp(scores - lse)
+        prob_grad = lax.dot_general(
+            keys, upstream, (((1,), (1,)), ((), ())), preferred_element_type=jnp.float32
+        )
+        score_grad = (probs * (prob_grad - delta)).astype(jnp.bfloat16)
+        dkv_ref[here] += jnp.dot(
+            score_grad, queries, preferred_element_type=jnp.float32
+        ) + jnp.dot(probs.astype(jnp.bfloat16), upstream, preferred_element_type=jnp.float32)
+        return query_grad + jnp.dot(
+            kvt_ref[:, here], score_grad, preferred_element_type=jnp.float32
+        )
+
+    masked_step = functools.partial(step, masked=True)
+    grad = jnp.zeros((128, QUERY_BLOCK), jnp.float32)
+    grad = lax.fori_loop(plan_ref[0, i], plan_ref[1, i], masked_step, grad)
+    grad = lax.fori_loop(
+        plan_ref[1, i], plan_ref[2, i], functools.partial(step, masked=False), grad
+    )
+    grad = lax.fori_loop(plan_ref[2, i], plan_ref[3, i], masked_step, grad)
+    dq_ref[...] = jnp.transpose(grad)
+
+
+def attend_back(plan, query_start, queries, upstream, pairs, low, end, lse, delta):
+    count = queries.shape[0]
+    blocks = count // QUERY_BLOCK
+    rows = [
+        jnp.broadcast_to(low[None], (8, count)),
+        jnp.broadcast_to(end[None], (8, count)),
+        lse,
+        jnp.broadcast_to(delta[None], (8, count)),
+    ]
+    wide = pl.BlockSpec((QUERY_BLOCK, 128), lambda i, *_: (i, 0))
+    row = pl.BlockSpec((8, QUERY_BLOCK), lambda i, *_: (0, i))
+    whole = pl.BlockSpec(pairs.shape, lambda i, *_: (0, 0))
+    flat = pl.BlockSpec(pairs.shape[::-1], lambda i, *_: (0, 0))
+    return pl.pallas_call(
+        attend_back_kernel,
+        out_shape=[
+            jax.ShapeDtypeStruct((count, 128), jnp.float32),
+            jax.ShapeDtypeStruct(pairs.shape, jnp.float32),
+        ],
+        grid_spec=pltpu.PrefetchScalarGridSpec(
+            num_scalar_prefetch=2,
+            grid=(blocks,),
+            in_specs=[wide, wide, whole, flat, row, row, row, row],
+            out_specs=[wide, whole],
+        ),
+        compiler_params=pltpu.CompilerParams(vmem_limit_bytes=56 * 2**20),
+    )(plan, query_start, queries, upstream, pairs, pairs.T, *rows)
 
 
 MESH = pl.DeviceIdType.MESH
@@ -105,7 +292,8 @@
 def gather_kernel(shapes, targets, n_out, *refs):
     n = len(shapes)
     ins, outs = (refs[:n], refs[n : n + n_out])
-    send, recv, own = refs[n + n_out :]
+    send, recv, own_in, own_out = refs[n + n_out : n + n_out + 4]
+    bounce = refs[n + n_out + 4 :]
     shard, _, core, _, _ = place()
     greet(("xb", "core") + GATHER_DIMS)
     sent = []
@@ -117,13 +305,14 @@
     locals_ = []
     for i, (rows, cols) in enumerate(shapes):
         out, off = targets[i]
-        copy = pltpu.make_async_copy(
-            ins[i],
+        inward = pltpu.make_async_copy(ins[i], bounce[i], own_in.at[i])
+        inward.start()
+        outward = pltpu.make_async_copy(
+            bounce[i],
             outs[out].at[pl.ds(pl.multiple_of(shard * rows, rows), rows), pl.ds(off, cols)],
-            own.at[i],
-        )
-        copy.start()
-        locals_.append(copy)
+            own_out.at[i],
+        )
+        locals_.append((inward, outward))
 
     def block(i, part, base, at, size, inner=False):
         rows, cols = shapes[i]
@@ -152,6 +341,9 @@
             )
             start(copy)
             plan[i, part] = (order, starts, copy)
+    for inward, outward in locals_:
+        inward.wait()
+        outward.start()
     siblings = []
     for stage in range(1, 6):
         for i, (rows, _) in enumerate(shapes):
@@ -180,8 +372,8 @@
         copy.wait_recv()
     for copy in sent:
         copy.wait_send()
-    for copy in locals_:
-        copy.wait()
+    for _, outward in locals_:
+        outward.wait()
 
 
 def gather_weights(arrays, targets, out_shapes, collective_id):
@@ -196,8 +388,12 @@
             pltpu.SemaphoreType.DMA((n, 4, 7)),
             pltpu.SemaphoreType.DMA((n, 4, 7)),
             pltpu.SemaphoreType.DMA((n,)),
+            pltpu.SemaphoreType.DMA((n,)),
+            *[pltpu.VMEM(shape, jnp.bfloat16) for shape in shapes],
         ],
-        compiler_params=pltpu.CompilerParams(collective_id=collective_id, has_side_effects=True),
+        compiler_params=pltpu.CompilerParams(
+            collective_id=collective_id, has_side_effects=True, vmem_limit_bytes=40 * 2**20
+        ),
     )(*arrays)
 
 
@@ -486,22 +682,59 @@
     return jax.nn.gelu(values, approximate=False)
 
 
-def allowed_mask(segments, valid, query_start, key_start, query_count, key_count):
-    seg_query = lax.dynamic_slice_in_dim(segments, query_start, query_count)
-    seg_key = lax.dynamic_slice_in_dim(segments, key_start, key_count)
-    live_key = lax.dynamic_slice_in_dim(valid, key_start, key_count)
-    place_query = query_start + jnp.arange(query_count, dtype=jnp.int32)
-    place_key = key_start + jnp.arange(key_count, dtype=jnp.int32)
-    same_doc = (seg_query[:, None] == seg_key[None, :]) & (live_key[None, :] == 1)
-    return same_doc | (place_query[:, None] == place_key[None, :])
-
-
-def pass_keys(kv_pair):
-    return from_behind(kv_pair, "blk", 1)
-
-
-def pass_grads(grad_pair):
-    return from_behind(grad_pair.astype(jnp.bfloat16), "blk", 1).astype(grad_pair.dtype)
+def neighbour(value, bit):
+    flips = [(i, i ^ bit) for i in range(4)]
+    return lax.ppermute(value, "blk", flips)
+
+
+def project_kernel(x_ref, w_ref, o_ref):
+    for piece in range(2):
+        cols = pl.ds(piece * 512, 512)
+        q, k, v = [
+            jnp.dot(
+                x_ref[...],
+                w_ref[:, pl.ds(which * 1024 + piece * 512, 512)],
+                preferred_element_type=jnp.float32,
+            )
+            for which in range(3)
+        ]
+        q = (q.astype(jnp.bfloat16).astype(jnp.float32) * HEAD ** (-0.5)).astype(jnp.bfloat16)
+        k, v = (k.astype(jnp.bfloat16), v.astype(jnp.bfloat16))
+        for h in range(8):
+            at = slice(h * HEAD, (h + 1) * HEAD)
+            head = piece * 8 + h
+            o_ref[head, 0:128] = jnp.concatenate([k[:, at], v[:, at]], axis=1)
+            o_ref[head, 128:192] = jnp.concatenate([q[0:64, at], q[64:128, at]], axis=1)
+
+
+def project(token_rows, full_qkv):
+    return pl.pallas_call(
+        project_kernel,
+        out_shape=jax.ShapeDtypeStruct((HEADS, 192, 128), jnp.bfloat16),
+        compiler_params=pltpu.CompilerParams(vmem_limit_bytes=32 * 2**20),
+    )(token_rows, full_qkv)
+
+
+def unfold(packed):
+    n = packed.shape[0]
+    return packed.reshape(n, 64, 2, HEAD).transpose(0, 2, 1, 3).reshape(n * 128, HEAD)
+
+
+def fold(rows):
+    n = rows.shape[0] // 128
+    return rows.reshape(n, 2, 64, HEAD).transpose(0, 2, 1, 3).reshape(n, 64, 2 * HEAD)
+
+
+def to_tokens(packed):
+    return packed.reshape(HEADS, 64, 2, HEAD).transpose(2, 1, 0, 3).reshape(128, HEADS * HEAD)
+
+
+def to_heads(rows):
+    return rows.reshape(2, 64, HEADS, HEAD).transpose(2, 1, 0, 3).reshape(HEADS, 64, 2 * HEAD)
+
+
+def swap(packed):
+    return lax.all_to_all(packed, "aa", split_axis=0, concat_axis=0, tiled=True)
 
 
 def shards(
@@ -529,91 +762,23 @@
         [(1024, 3072), (1024, 1024), (1024, 4096), (4096, 1024)],
         0,
     )
-    full_query, full_key, full_value = jnp.split(full_qkv, 3, axis=1)
-    norms = lax.all_gather(packed, "shard", axis=1, tiled=True)[:4]
+    norms = lax.all_gather(packed, "shard", axis=1, tiled=True)[:4].astype(jnp.float32)
     gain_one, bias_one, gain_two, bias_two = norms
-    gain_one = gain_one.astype(jnp.float32)
-    bias_one = bias_one.astype(jnp.float32)
-    gain_two = gain_two.astype(jnp.float32)
-    bias_two = bias_two.astype(jnp.float32)
     token_rows = tokens[0]
-    seq_segments = segments[0]
-    seq_valid = valid[0]
-    tok_rows, width = token_rows.shape
-    groups = lax.axis_size("aa")
-    head_local = HEADS // groups
-    group_width = head_local * HEAD
-    block_len = groups * tok_rows
-    block_count = block_len // QBLK
-    score_scale = HEAD ** (-0.5)
-    cycle_size = lax.axis_size("blk")
-    cycle_index = lax.axis_index("blk")
-    query_base = cycle_index * block_len
-    block_ids = jnp.arange(block_count, dtype=jnp.int32)
-    projected = [
-        jnp.dot(token_rows, matrix, preferred_element_type=jnp.float32)
-        .astype(jnp.bfloat16)
-        .reshape(tok_rows, groups, group_width)
-        for matrix in (full_query, full_key, full_value)
-    ]
-    heads_all = lax.all_to_all(
-        jnp.concatenate(projected, axis=2), "aa", split_axis=1, concat_axis=0, tiled=True
-    )
-    heads_all = heads_all.reshape(block_len, 3, head_local, HEAD)
-    q_blocks = heads_all[:, 0].reshape(block_count, QBLK, head_local, HEAD)
-    kv_pair = heads_all[:, 1:]
-    state = (
-        jnp.full((block_count, head_local, QBLK), MASKED_SCORE, jnp.float32),
-        jnp.zeros((block_count, head_local, QBLK), jnp.float32),
-        jnp.zeros((block_count, QBLK, head_local, HEAD), jnp.float32),
-    )
-    kept_pairs = []
-    for cycle_step in range(cycle_size):
-        if cycle_step > 0:
-            kv_pair = pass_keys(kv_pair)
-        kept_pairs.append(kv_pair)
-        key_start = (cycle_index - cycle_step) % cycle_size * block_len
-        attend_key_heads = kv_pair[:, 0]
-        attend_value_heads = kv_pair[:, 1]
-
-        def attend_visit(inputs):
-            block_index, query_block, running_max, running_sum, summed = inputs
-            allowed = allowed_mask(
-                seq_segments, seq_valid, query_base + block_index * QBLK, key_start, QBLK, block_len
-            )
-            scores = (
-                jnp.einsum(
-                    "qhd,khd->hqk",
-                    query_block,
-                    attend_key_heads,
-                    preferred_element_type=jnp.float32,
-                )
-                * score_scale
-            )
-            scores = jnp.where(allowed[None], scores, MASKED_SCORE)
-            new_max = jnp.maximum(running_max, jnp.max(scores, axis=-1))
-            factor = jnp.exp(running_max - new_max)
-            weights_new = jnp.exp(scores - new_max[..., None])
-            new_sum = running_sum * factor + jnp.sum(weights_new, axis=-1)
-            new_summed = summed * jnp.transpose(factor)[..., None] + jnp.einsum(
-                "hqk,khd->qhd",
-                weights_new.astype(jnp.bfloat16),
-                attend_value_heads,
-                preferred_element_type=jnp.float32,
-            )
-            return (new_max, new_sum, new_summed)
-
-        state = lax.map(attend_visit, (block_ids, q_blocks) + state)
-    running_max, running_sum, summed = state
-    attn_heads = summed / jnp.transpose(running_sum, (0, 2, 1))[..., None]
-    log_total = running_max + jnp.log(running_sum)
-    mixed = lax.all_to_all(
-        attn_heads.astype(jnp.bfloat16).reshape(block_len, 1, group_width),
-        "aa",
-        split_axis=0,
-        concat_axis=1,
-        tiled=True,
-    ).reshape(tok_rows, width)
+    blk = lax.axis_index("blk")
+    query_start = blk * BLOCK_LEN
+    place = jnp.stack([query_start, blk]).astype(jnp.int32)
+    plan, low, end = block_plan(*spans(segments[0], valid[0]), query_start, BLOCK_LEN)
+
+    heads_all = swap(project(token_rows, full_qkv))
+    own_pair = heads_all[:, 0:128].reshape(BLOCK_LEN, 128)
+    queries = jnp.pad(unfold(heads_all[:, 128:192]), ((0, 0), (0, HEAD)))
+    far_pair = neighbour(own_pair, 2)
+    pairs = jnp.concatenate([own_pair, neighbour(own_pair, 1), far_pair, neighbour(far_pair, 1)])
+    summed, lse = attend(plan, place, queries, pairs, low, end)
+    attn_heads = summed[:, HEAD:]
+    mixed = to_tokens(swap(fold(attn_heads.astype(jnp.bfloat16))))
+
     attn = jnp.dot(mixed, full_out, preferred_element_type=jnp.float32)
     first, scaled_one, inv_one = normalize(
         token_rows.astype(jnp.float32) + attn, gain_one, bias_one
@@ -636,8 +801,29 @@
         first_grad, scaled_one, inv_one, gain_one
     )
     attn_grad = grad_one.astype(jnp.bfloat16)
+    mixed_grad = jnp.einsum(
+        "td,cd->tc", attn_grad, full_out, preferred_element_type=jnp.float32
+    ).astype(jnp.bfloat16)
     norm_sums = jnp.stack([grad_gain_one, grad_bias_one, grad_gain_two, grad_bias_two])
     norm_sums = jnp.pad(norm_sums.reshape(4, 2, 512).transpose(1, 0, 2), ((0, 0), (0, 4), (0, 0)))
+
+    head_grads = unfold(swap(to_heads(mixed_grad)))
+    delta = jnp.sum(head_grads.astype(jnp.float32) * attn_heads, axis=-1)
+    wide_grads = jnp.pad(head_grads, ((0, 0), (HEAD, 0)))
+    query_grad, pair_grads = attend_back(
+        plan, place, queries, wide_grads, pairs, low, end, lse, delta
+    )
+    pair_grads = pair_grads.reshape(4, BLOCK_LEN, 128)
+    theirs = neighbour(pair_grads[1::2].astype(jnp.bfloat16), 1).astype(jnp.float32)
+    near = pair_grads[0::2] + theirs
+    own_grad = near[0] + neighbour(near[1].astype(jnp.bfloat16), 2).astype(jnp.float32)
+    query_grad = fold((query_grad[:, :HEAD] * HEAD ** (-0.5)).astype(jnp.bfloat16))
+    own_grad = own_grad.astype(jnp.bfloat16).reshape(16, 128, 128)
+    token_grads = swap(jnp.concatenate([own_grad, query_grad], axis=1))
+    query_tok = to_tokens(token_grads[:, 128:192])
+    key_tok = token_grads[:, 0:128, :HEAD].transpose(1, 0, 2).reshape(128, 1024)
+    value_tok = token_grads[:, 0:128, HEAD:].transpose(1, 0, 2).reshape(128, 1024)
+
     ff_summed, norm_total = reduce_gradients(
         [first_low, hidden, mixed],
         [pre_grad, ff_grad, attn_grad],
@@ -646,94 +832,10 @@
         norm_sums,
         1,
     )
-    grad_in, grad_down, grad_out_weight = ff_grads_out(ff_summed)
-    mixed_grad = jnp.einsum(
-        "td,cd->tc", attn_grad, full_out, preferred_element_type=jnp.float32
-    ).astype(jnp.bfloat16)
-    grad_blocks = lax.all_to_all(
-        mixed_grad.reshape(tok_rows, groups, group_width),
-        "aa",
-        split_axis=1,
-        concat_axis=0,
-        tiled=True,
-    )
-    grad_blocks = grad_blocks.reshape(block_count, QBLK, head_local, HEAD)
-    delta = jnp.transpose(jnp.sum(grad_blocks.astype(jnp.float32) * attn_heads, axis=-1), (0, 2, 1))
-    grad_pair = jnp.zeros((block_len, 2, head_local, HEAD), jnp.float32)
-    query_grad = jnp.zeros((block_count, QBLK, head_local, HEAD), jnp.float32)
-    for cycle_step in range(cycle_size):
-        if cycle_step > 0:
-            grad_pair = pass_grads(grad_pair)
-        key_start = (cycle_index - cycle_step) % cycle_size * block_len
-        current_pair = kept_pairs[cycle_step]
-        key_heads = current_pair[:, 0]
-        value_heads = current_pair[:, 1]
-
-        def visit(carry, inputs):
-            block_index, query_block, grad_block, log_block, delta_block = inputs
-            allowed = allowed_mask(
-                seq_segments, seq_valid, query_base + block_index * QBLK, key_start, QBLK, block_len
-            )
-            scores = (
-                jnp.einsum(
-                    "qhd,khd->hqk", query_block, key_heads, preferred_element_type=jnp.float32
-                )
-                * score_scale
-            )
-            scores = jnp.where(allowed[None], scores, MASKED_SCORE)
-            probs = jnp.exp(scores - log_block[..., None])
-            value_part = jnp.einsum(
-                "hqk,qhd->khd",
-                probs.astype(jnp.bfloat16),
-                grad_block,
-                preferred_element_type=jnp.float32,
-            )
-            prob_grad = jnp.einsum(
-                "qhd,khd->hqk", grad_block, value_heads, preferred_element_type=jnp.float32
-            )
-            score_grad = (probs * (prob_grad - delta_block[..., None])).astype(jnp.bfloat16)
-            query_part = (
-                jnp.einsum(
-                    "hqk,khd->qhd", score_grad, key_heads, preferred_element_type=jnp.float32
-                )
-                * score_scale
-            )
-            key_part = (
-                jnp.einsum(
-                    "hqk,qhd->khd", score_grad, query_block, preferred_element_type=jnp.float32
-                )
-                * score_scale
-            )
-            return (carry + jnp.stack([key_part, value_part], axis=1), query_part)
-
-        grad_pair, query_part = lax.scan(
-            visit, grad_pair, (block_ids, q_blocks, grad_blocks, log_total, delta)
-        )
-        query_grad = query_grad + query_part
-    grad_pair = pass_grads(grad_pair)
-    head_grads = jnp.concatenate(
-        [query_grad.reshape(block_len, 1, head_local, HEAD), grad_pair], axis=1
-    ).astype(jnp.bfloat16)
-    token_grads = lax.all_to_all(
-        head_grads.reshape(block_len, 1, 3 * group_width),
-        "aa",
-        split_axis=0,
-        concat_axis=1,
-        tiled=True,
-    )
-    token_grads = token_grads.reshape(tok_rows, groups, 3, group_width)
-    query_tok = token_grads[:, :, 0].reshape(tok_rows, width)
-    key_tok = token_grads[:, :, 1].reshape(tok_rows, width)
-    value_tok = token_grads[:, :, 2].reshape(tok_rows, width)
-    input_grad = grad_one
-    input_grad = input_grad + jnp.einsum(
-        "td,cd->tc", query_tok, full_query, preferred_element_type=jnp.float32
-    )
-    input_grad = input_grad + jnp.einsum(
-        "td,cd->tc", key_tok, full_key, preferred_element_type=jnp.float32
-    )
-    input_grad = input_grad + jnp.einsum(
-        "td,cd->tc", value_tok, full_value, preferred_element_type=jnp.float32
+    grad_in, grad_down, grad_out = ff_grads_out(ff_summed)
+    all_tok = jnp.concatenate([query_tok, key_tok, value_tok], axis=1)
+    input_grad = grad_one + jnp.einsum(
+        "td,cd->tc", all_tok, full_qkv, preferred_element_type=jnp.float32
     )
     qkv_summed = reduce_gradients(
         [token_rows], [query_tok, key_tok, value_tok], QKV_DOTS, QKV_WIDTHS, None, 2
@@ -744,7 +846,7 @@
         square_out(qkv_summed, 0),
         square_out(qkv_summed, 1),
         square_out(qkv_summed, 2),
-        grad_out_weight,
+        grad_out,
         norm_total[0],
         norm_total[1],
         grad_in,

time: 959 us -> 491 us (0.51)
  Pallas kernels: 584 us -> 330 us
  matrix products: 168 us -> 26.9 us
  loops' own time: 23 us -> 0 us
  other arithmetic: 36.2 us -> 15.6 us
  local copies, waits for them, and re-layouts: 53.9 us -> 35.6 us
  blocking collectives: 5.47 us -> 21.5 us
  starting transfers between devices: 32.5 us -> 17 us
    pallas_call x1, Pallas kernels: 390 us -> 56.6 us  [gather_weights(): pl.pallas_call(functools.partial(gather_kernel, shapes, targets, len(out_...]
    dot_general x118 -> x1, matrix products: 146 us -> 5.68 us  [shards(): jnp.einsum('td,cd->tc', all_tok, full_qkv, preferred_element_type=jnp.flo...]
    pallas_call x0 -> x3, Pallas kernels: none -> 79.1 us  [the longest x1 43.5 us: attend_back(): pl.pallas_call(attend_back_kernel, out_shape=[jax.ShapeDtypeStruct((count...]
    another operation x8 -> x0, loops' own time: 23 us -> none  [the longest x4 11.6 us: shards(): lax.scan(visit, grad_pair, (block_ids, q_blocks, grad_blocks, log_total,...]
    dynamic_slice x81 -> x1, local copies, waits for them, and re-layouts: 21.7 us -> 0.01 us  [block_plan(): lax.dynamic_slice_in_dim(a, query_start, count)]
    add x81 -> x1, other arithmetic: 11.4 us -> 0.24 us  [shards(): near = pair_grads[0::2] + theirs]
    all_to_all x0 -> x1, blocking collectives: none -> 10.6 us  [swap(): return lax.all_to_all(packed, 'aa', split_axis=0, concat_axis=0, tiled=True)]
    ppermute x7 -> x5, waiting for transfers between devices: 23 us -> 14.1 us  [neighbour(): return lax.ppermute(value, 'blk', flips)]
  transfers between devices with their start and end apart: 11 -> 8, of which waited for: 7 -> 4; matrix products, arithmetic and copies ran while one was open for 6% -> 2% of each run, Pallas kernels for 13% -> 26%
where the time goes in v2:
time: 491 us; the launch traced here: 484 us
  Pallas kernels  330 us (67%)
  local copies, waits for them, and re-layouts  35.6 us (7%)
  waiting for transfers between devices  35.5 us (7%)
  matrix products  26.9 us (5%)
  blocking collectives  21.5 us (4%)
  starting transfers between devices  17 us (3%)
  other arithmetic  15.6 us (3%)
    pallas_call x2, Pallas kernels, reduce_gradients(): pl.pallas_call(functools.partial(reduce_kernel, len(lefts), dots, widths,...  170 us
    pallas_call x1, Pallas kernels, gather_weights(): pl.pallas_call(functools.partial(gather_kernel, shapes, targets, len(out_...  56.6 us
    pallas_call x1, Pallas kernels, attend_back(): pl.pallas_call(attend_back_kernel, out_shape=[jax.ShapeDtypeStruct((count...  43.5 us
    pallas_call x1, Pallas kernels, attend(): pl.pallas_call(attend_kernel, out_shape=[jax.ShapeDtypeStruct((count, 128...  33.6 us
    pallas_call x6, Pallas kernels, cast_out(): pl.pallas_call(cast_kernel, out_shape=jax.ShapeDtypeStruct(shape, jnp.flo...  24.4 us
    all_to_all x3, waiting for transfers between devices, swap(): return lax.all_to_all(packed, 'aa', split_axis=0, concat_axis=0, tiled=True)  21.4 us
    ppermute x5, waiting for transfers between devices, neighbour(): return lax.ppermute(value, 'blk', flips)  14.1 us
    all_to_all x3, starting transfers between devices, swap(): return lax.all_to_all(packed, 'aa', split_axis=0, concat_axis=0, tiled=True)  11.8 us
  transfers between devices with their start and end apart: 8, of which 4 were waited for; matrix products, arithmetic and copies ran while one was open for 2% of the time, Pallas kernels for 26%

profile of v2, /device:TPU:1, one launch (start us, length us, event | category | flops | bytes accessed | tf_op | source)
XLA Modules:
  0.0 484.2 jit_solution(15894403845215457257)
XLA Ops:
  7.7 56.6 %shard_map.229 = (bf16[1024,3072]{1,0:T(8,128)(2,1)}, bf16[1024,1024]{1,0:T(8,128)(2,1)S(1)}, bf16[1024,4096]{1,0:T(8,128)(2,1)}, bf16[4096,1024]{1,0:T(8,128)(2,1)}) custom-call(bf16[512,1024]{1,0:T(8,128)(2,1)S(1)} %copy-done.3, bf16[512,1024]{1,0:T(8,128)(2,1)S(1)} %copy-done.4, bf16[512,1024]{1,0:T(8,128)(2,1)S(1)} %copy-done.5, ...), custom_call_target="tpu_custom_call" | custom-call | tf_op jit(solution)/shard_map/pallas_call | solution.py:382
  64.4 2.8 copy-done
  69.2 4.5 all-to-all-start
  73.9 13.9 %all-to-all-done = bf16[16,192,128]{2,1,0:T(8,128)(2,1)S(1)} async-done(((bf16[16,192,128]{2,1,0:T(8,128)(2,1)}), bf16[16,192,128]{2,1,0:T(8,128)(2,1)S(1)}, u32[]{:S(2)}, u32[]{:S(2)}) %all-to-all-start) | async-done | bytes 786464 | tf_op jit(solution)/shard_map/all_to_all | solution.py:737
  92.7 10.9 %all_gather.3 = bf16[16,1024]{1,0:T(8,128)(2,1)S(1)} all-gather(bf16[16,512]{1,0:T(8,128)(2,1)S(1)} %fusion.35), channel_id=1, replica_groups=mesh['shard'=2,'blk'=4,'aa'=16] {'shard'}, dimensions={1}, use_global_device_ids=true | all-gather | bytes 49152 | tf_op jit(solution)/shard_map/all_gather | solution.py:765
  111.1 3.9 fusion.42
  115.0 4.1 copy.66.kv_ref
  120.3 33.6 %shard_map.231 = (f32[2048,128]{1,0:T(8,128)}, f32[8,2048]{1,0:T(8,128)}) custom-call(s32[4,4]{1,0:T(4,128)} %pad_add_fusion.plan_ref, s32[2]{0:T(128)} %pad_add_fusion.1.start_ref, bf16[2048,128]{1,0:T(8,128)(2,1)} %pad.15.q_ref, bf16[8192,128]{1,0:T(8,128)(2,1)} %copy.66.kv_ref, bf16[128,8192]{1,0:T(8,128)(2,1)} %get-tuple-element.61.kvt_ref, ...), custom_call_target="tpu_custom_call" | custom-call | tf_op jit(solution)/shard_map/pallas_call | solution.py:107
  156.8 3.5 all-to-all-start.1
  160.4 7.5 %all-to-all-done.1 = bf16[16,64,128]{2,1,0:T(8,128)(2,1)S(1)} async-done(((bf16[16,64,128]{2,1,0:T(8,128)(2,1)}), bf16[16,64,128]{2,1,0:T(8,128)(2,1)S(1)}, u32[]{:S(2)}, u32[]{:S(2)}) %all-to-all-start.1) | async-done | bytes 262176 | tf_op jit(solution)/shard_map/all_to_all | solution.py:737
  169.8 9.5 %multiply_convert_fusion = (bf16[128,4096]{1,0:T(8,128)(2,1)S(1)}, f32[128,4096]{1,0:T(8,128)}, f32[128,4096]{1,0:T(8,128)}) fusion(bf16[128,1024]{1,0:T(8,128)(2,1)S(1)} %fusion.27.refs_0_, bf16[1024,4096]{1,0:T(8,128)(2,1)} %get-tuple-element.37), kind=kOutput, calls=%fused_computation.5 | convolution fusion | flops 1107820544 | bytes 13893632 | tf_op jit(solution)/shard_map/dot_general | solution.py:787
  182.4 5.8 %add_convert_fusion.refs_3_ = bf16[128,4096]{1,0:T(8,128)(2,1)S(1)} fusion(f32[128,4096]{1,0:T(8,128)} %get-tuple-element.58, f32[128,4096]{1,0:T(8,128)} %get-tuple-element.83, bf16[128,1024]{1,0:T(8,128)(2,1)S(1)} %get-tuple-element.65.refs_4_, bf16[4096,1024]{1,0:T(8,128)(2,1)S(1)} %bitcast.169), kind=kOutput, calls=%fused_computation.4 | convolution fusion | flops 1081081856 | bytes 13893632 | tf_op jit(solution)/shard_map/td,fd->tf/dot_general | solution.py:794
  188.2 3.1 multiply_reduce_fusion.1
  194.4 10.6 %all_to_all.20 = bf16[16,64,128]{2,1,0:T(8,128)(2,1)S(1)} all-to-all(bf16[16,64,128]{2,1,0:T(8,128)(2,1)S(1)} %reshape.510), channel_id=1, replica_groups=mesh['shard'=2,'blk'=4,'aa'=16] {'aa'}, dimensions={0} | all-to-all | bytes 524288 | tf_op jit(solution)/shard_map/all_to_all | solution.py:737
  207.6 43.5 %shard_map.232 = (f32[2048,128]{1,0:T(8,128)}, f32[8192,128]{1,0:T(8,128)}) custom-call(s32[4,4]{1,0:T(4,128)} %pad_add_fusion.plan_ref, s32[2]{0:T(128)} %pad_add_fusion.1.start_ref, bf16[2048,128]{1,0:T(8,128)(2,1)} %pad.15.q_ref, bf16[2048,128]{1,0:T(8,128)(2,1)} %pad.16.g_ref, bf16[8192,128]{1,0:T(8,128)(2,1)} %copy.66.kv_ref, ...), custom_call_target="tpu_custom_call" | custom-call | tf_op jit(solution)/shard_map/pallas_call | solution.py:196
  251.2 2.6 convert.6
  254.0 2.6 collective-permute-done.3
  260.8 11.4 %collective-permute-done.4 = bf16[2048,128]{1,0:T(8,128)(2,1)} collective-permute-done((bf16[2048,128]{1,0:T(8,128)(2,1)}, bf16[2048,128]{1,0:T(8,128)(2,1)}, u32[]{:S(2)}, u32[]{:S(2)}) %collective-permute-start.4) | collective-permute-done | bytes 524320 | tf_op jit(solution)/shard_map/ppermute | solution.py:687
  274.3 3.8 all-to-all-start.3
  278.8 108.7 %shard_map.237 = (bf16[2,512,4608]{2,1,0:T(8,128)(2,1)}, f32[8,512]{1,0:T(8,128)}) custom-call(bf16[128,1024]{1,0:T(8,128)(2,1)} %copy-done.17, bf16[128,4096]{1,0:T(8,128)(2,1)} %copy-done.8, bf16[128,1024]{1,0:T(8,128)(2,1)} %copy-done.13, bf16[128,4096]{1,0:T(8,128)(2,1)} %copy-done.9, bf16[128,1024]{1,0:T(8,128)(2,1)} %copy-done.15, ...), custom_call_target="tpu_custom_call" | custom-call | tf_op jit(solution)/shard_map/pallas_call | solution.py:616
  389.9 7.3 %shard_map.239 = f32[512,4096]{1,0:T(8,128)} custom-call(bf16[2,512,4608]{2,1,0:T(8,128)(2,1)} %get-tuple-element.42.x_ref), custom_call_target="tpu_custom_call" | custom-call | tf_op jit(solution)/shard_map/pallas_call | solution.py:643
  397.2 7.3 %shard_map.240 = f32[2048,1024]{1,0:T(8,128)} custom-call(bf16[2,512,4608]{2,1,0:T(8,128)(2,1)} %get-tuple-element.42.x_ref), custom_call_target="tpu_custom_call" | custom-call | tf_op jit(solution)/shard_map/pallas_call | solution.py:643
  409.2 61.7 %shard_map.233.x_ref = bf16[2,512,1536]{2,1,0:T(8,128)(2,1)} custom-call(bf16[128,1024]{1,0:T(8,128)(2,1)} %bitcast.166, bf16[128,1024]{1,0:T(8,128)(2,1)} %reshape.518.refs_1_, bf16[128,1024]{1,0:T(8,128)(2,1)} %copy.76.refs_2_, bf16[128,1024]{1,0:T(8,128)(2,1)} %copy.77.refs_3_), custom_call_target="tpu_custom_call" | custom-call | tf_op jit(solution)/shard_map/pallas_call | solution.py:616
  478.3 5.7 %fusion.9 = bf16[1,128,1024]{2,1,0:T(8,128)(2,1)} fusion(f32[128,1024]{1,0:T(8,128)S(1)} %copy-done.21, bf16[1024,3072]{1,0:T(8,128)(2,1)} %get-tuple-element.34.w_ref, bf16[128,1024]{1,0:T(8,128)(2,1)S(1)} %copy-done.18, bf16[128,1024]{1,0:T(8,128)(2,1)S(1)} %copy-done.19, bf16[128,1024]{1,0:T(8,128)(2,1)S(1)} %copy-done.16), kind=kOutput, calls=%fused_computation.31 | convolution fusion | flops 807927808 | bytes 7864320 | tf_op jit(solution)/shard_map/td,cd->tc/dot_general | solution.py:837
  (163 shorter events, 57.7 us)
Async XLA Ops:
  7.7 56.6 %copy-start.2 = (bf16[1,128,1024]{2,1,0:T(8,128)(2,1)S(1)}, bf16[1,128,1024]{2,1,0:T(8,128)(2,1)}, u32[]{:S(2)}) copy-start(bf16[1,128,1024]{2,1,0:T(8,128)(2,1)} %param.16) | copy-start | bytes 786436
  67.2 6.5 %copy-start.22 = (s32[1,8192]{1,0:T(1,128)S(1)}, s32[1,8192]{1,0:T(1,128)}, u32[]{:S(2)}) copy-start(s32[1,8192]{1,0:T(1,128)} %param.17) | copy-start | bytes 98308
  69.1 22.1 %copy-start.23 = (s32[1,8192]{1,0:T(1,128)S(1)}, s32[1,8192]{1,0:T(1,128)}, u32[]{:S(2)}) copy-start(s32[1,8192]{1,0:T(1,128)} %param.18) | copy-start | bytes 98308
  69.1 23.5 %copy-start.25 = (bf16[512]{0:T(512)(128)(2,1)S(1)}, bf16[512]{0:T(512)(128)(2,1)}, u32[]{:S(2)}) copy-start(bf16[512]{0:T(512)(128)(2,1)} %param.28) | copy-start | bytes 3076
  69.1 23.5 %copy-start.26 = (bf16[512]{0:T(512)(128)(2,1)S(1)}, bf16[512]{0:T(512)(128)(2,1)}, u32[]{:S(2)}) copy-start(bf16[512]{0:T(512)(128)(2,1)} %param.27) | copy-start | bytes 3076
  69.1 23.5 %copy-start.27 = (bf16[512]{0:T(512)(128)(2,1)S(1)}, bf16[512]{0:T(512)(128)(2,1)}, u32[]{:S(2)}) copy-start(bf16[512]{0:T(512)(128)(2,1)} %param.24) | copy-start | bytes 3076
  69.2 23.5 %copy-start.28 = (bf16[512]{0:T(512)(128)(2,1)S(1)}, bf16[512]{0:T(512)(128)(2,1)}, u32[]{:S(2)}) copy-start(bf16[512]{0:T(512)(128)(2,1)} %param.23) | copy-start | bytes 3076
  69.2 18.7 %all-to-all-start = ((bf16[16,192,128]{2,1,0:T(8,128)(2,1)}), bf16[16,192,128]{2,1,0:T(8,128)(2,1)S(1)}, u32[]{:S(2)}, u32[]{:S(2)}) async-start(bf16[16,192,128]{2,1,0:T(8,128)(2,1)} %shard_map.230), calls=%async_computation | async-start | bytes 1572864 | tf_op jit(solution)/shard_map/all_to_all | solution.py:737
  90.7 15.7 %collective-permute-start.1 = (bf16[2048,128]{0,1:T(8,128)(2,1)}, bf16[2048,128]{0,1:T(8,128)(2,1)}, u32[]{:S(2)}, u32[]{:S(2)}) collective-permute-start(bf16[2048,128]{0,1:T(8,128)(2,1)} %copy.80), channel_id=1, source_target_pairs={{0,32},{16,48},{32,0},{48,16},{1,33},{17,49},{33,1},{49,17},{2,34}... | collective-permute-start | bytes 1572872 | tf_op jit(solution)/shard_map/ppermute | solution.py:687
  103.8 7.3 %collective-permute-start = (bf16[2048,128]{0,1:T(8,128)(2,1)}, bf16[2048,128]{0,1:T(8,128)(2,1)}, u32[]{:S(2)}, u32[]{:S(2)}) collective-permute-start(bf16[2048,128]{0,1:T(8,128)(2,1)} %copy.80), channel_id=1, source_target_pairs={{0,16},{16,0},{32,48},{48,32},{1,17},{17,1},{33,49},{49,33},{2,18}... | collective-permute-start | bytes 1572872 | tf_op jit(solution)/shard_map/ppermute | solution.py:687
  106.4 4.7 collective-permute-start.2
  156.8 11.1 %all-to-all-start.1 = ((bf16[16,64,128]{2,1,0:T(8,128)(2,1)}), bf16[16,64,128]{2,1,0:T(8,128)(2,1)S(1)}, u32[]{:S(2)}, u32[]{:S(2)}) async-start(bf16[16,64,128]{2,1,0:T(8,128)(2,1)} %reshape.506), calls=%async_computation.1 | async-start | bytes 524288 | tf_op jit(solution)/shard_map/all_to_all | solution.py:737
  169.4 10.0 %slice-start = ((s8[8388608]{0:T(1024)(128)(4,1)}), s8[4194304]{0:T(1024)(128)(4,1)S(1)}, s32[]{:S(2)}) async-start(s8[8388608]{0:T(1024)(128)(4,1)} %bitcast.168), calls=%async_computation.4 | async-start | bytes 8388608
  169.8 9.6 %copy-start.17 = (bf16[128,1024]{1,0:T(8,128)(2,1)}, bf16[128,1024]{1,0:T(8,128)(2,1)S(1)}, u32[]{:S(2)}) copy-start(bf16[128,1024]{1,0:T(8,128)(2,1)S(1)} %fusion.27.refs_0_) | copy-start | bytes 786436
  169.8 9.6 %slice-start.1 = ((s8[8388608]{0:T(1024)(128)(4,1)}), s8[4194304]{0:T(1024)(128)(4,1)S(1)}, s32[]{:S(2)}) async-start(s8[8388608]{0:T(1024)(128)(4,1)} %bitcast.168), calls=%async_computation.5 | async-start | bytes 8388608
  181.1 7.1 %slice-start.2 = ((s8[8388608]{0:T(1024)(128)(4,1)}), s8[4194304]{0:T(1024)(128)(4,1)S(1)}, s32[]{:S(2)}) async-start(s8[8388608]{0:T(1024)(128)(4,1)} %bitcast.172), calls=%async_computation.6 | async-start | bytes 8388608
  182.4 5.8 %copy-start.15 = (bf16[128,1024]{1,0:T(8,128)(2,1)}, bf16[128,1024]{1,0:T(8,128)(2,1)S(1)}, u32[]{:S(2)}) copy-start(bf16[128,1024]{1,0:T(8,128)(2,1)S(1)} %get-tuple-element.65.refs_4_) | copy-start | bytes 786436
  182.4 5.8 %slice-start.3 = ((s8[8388608]{0:T(1024)(128)(4,1)}), s8[4194304]{0:T(1024)(128)(4,1)S(1)}, s32[]{:S(2)}) async-start(s8[8388608]{0:T(1024)(128)(4,1)} %bitcast.172), calls=%async_computation.7 | async-start | bytes 8388608
  193.6 11.8 %copy-start.11 = (f32[2048,128]{1,0:T(8,128)S(1)}, f32[2048,128]{1,0:T(8,128)}, u32[]{:S(2)}) copy-start(f32[2048,128]{1,0:T(8,128)} %get-tuple-element.35) | copy-start | bytes 3145732
  253.9 6.0 %copy-start.20 = (f32[2048,128]{1,0:T(8,128)S(1)}, f32[2048,128]{1,0:T(8,128)}, u32[]{:S(2)}) copy-start(f32[2048,128]{1,0:T(8,128)} %get-tuple-element.41) | copy-start | bytes 3145732
  253.9 2.7 collective-permute-start.3
  257.7 14.5 %collective-permute-start.4 = (bf16[2048,128]{1,0:T(8,128)(2,1)}, bf16[2048,128]{1,0:T(8,128)(2,1)}, u32[]{:S(2)}, u32[]{:S(2)}) collective-permute-start(bf16[2048,128]{1,0:T(8,128)(2,1)} %fusion.26), channel_id=1, source_target_pairs={{0,32},{16,48},{32,0},{48,16},{1,33},{17,49},{33,1},{49,17},{2,34}... | collective-permute-start | bytes 1572872 | tf_op jit(solution)/shard_map/ppermute | solution.py:687
  274.3 130.8 %all-to-all-start.3 = ((bf16[16,192,128]{2,1,0:T(8,128)(2,1)}), bf16[16,192,128]{2,1,0:T(8,128)(2,1)S(1)}, u32[]{:S(2)}, u32[]{:S(2)}) async-start(bf16[16,192,128]{2,1,0:T(8,128)(2,1)} %pad_maximum_fusion.1), calls=%async_computation.3 | async-start | bytes 1572864 | tf_op jit(solution)/shard_map/all_to_all | solution.py:737
  397.2 7.3 %copy-start.24 = (f32[8,512]{1,0:T(8,128)S(1)}, f32[8,512]{1,0:T(8,128)}, u32[]{:S(2)}) copy-start(f32[8,512]{1,0:T(8,128)} %get-tuple-element.43) | copy-start | bytes 49156
  (17 other events, 36.9 us)
